TPU v7x, 32 devices: a whole 2x2x4 slice. The times are simulated.
32 devices in a mesh: groups: 2 (over y), blk: 4 (over z), head: 2 (over x), rep: 2 (over core).
Axes of the slice: x: 2, y: 2, z: 4, core: 2. Of those that a mesh axis runs over, the one named last changes fastest.
Arguments:
- merger_rows: bfloat16 [1536, 5120], P(('groups', 'blk')), parts along dimension 0, may hold values from -6 to 6
- out_weight: bfloat16 [5120, 8192], P('blk', ('head', 'rep')), may hold values from -0.078125 to 0.078125
- kv_weight: bfloat16 [8192, 2048], P(('head', 'rep')), may hold values from -0.09375 to 0.09375
- kv_bias: float32 [8, 256], P('head'), may hold values from -3 to 3
- merge_map: int32 [16, 96], P(('groups', 'blk', 'rep')), parts along dimension 0, may hold values from 0 to 95, each once within a row
- owner_map: int32 [192, 1], P(('groups', 'blk', 'rep')), parts along dimension 0, may hold values from 0 to 3; in each aligned block of 12 rows (0 to 11, 12 to 23, ...) at most 6 rows name the same one
- old_memory: bfloat16 [2048, 8, 8, 256], P(('groups', 'blk', 'rep'), None, 'head'), parts along dimension 0, may hold values from -4 to 4
- queries: bfloat16 [8, 8, 8, 1024], P(('groups', 'blk'), None, 'head'), parts along dimension 0, may hold values from -6 to 6
- retrieved: int32 [8, 32], P('groups'), parts along dimension 0, may hold values from 0 to 1119, as said below
Outputs:
- answer: bfloat16 [8, 8, 8, 1024], P(('groups', 'blk'), 'rep', 'head'), parts along dimension 0
- new_memory: bfloat16 [384, 8, 8, 256], P(('groups', 'blk', 'rep'), None, 'head'), parts along dimension 0
There are 2 independent parts, one for each index of `groups`. A program takes and returns all parts, laid end to end along the dimension named above; an argument that names none is the same for every part. Nothing has to cross between parts.
Inputs may be any that keep to these rules, and one draw needn't show every extreme that they name: `merge_map`: each row of a group g is a permutation of 0 to 95. `owner_map`: in each aligned block of 12 rows (the new units of one index of blk and rep) no value appears more than 6 times. `retrieved`: each row holds 32 distinct ids: 24 stored units below 1024, then 8 new units from 1024 on.
All inputs are finite; a program needn't handle non-finite values.
Results may differ from a plain program's by a relative error of at most 0.025.
Values may be sent and summed in bfloat16 or wider, within the bound.
A program may use at most 192 MiB of HBM per device.

v0:
```python
import math

import jax
import jax.numpy as jnp
from jax import lax
from jax.sharding import PartitionSpec as P

KVH = 8
UNIT_TOK = 8


def combined_all(array, axis, combine):
    everything = jax.tree.map(
        lambda part, kind: lax.all_gather(part.astype(kind), axis),
        array,
        jax.tree.map(lambda a: jnp.bfloat16 if a.dtype == jnp.float32 else a.dtype, array),
    )

    def take(k):
        return jax.tree.map(lambda part, own: part[k].astype(own.dtype), everything, array)

    return lax.fori_loop(
        1, lax.axis_size(axis), lambda k, so_far: combine(so_far, take(k)), take(0)
    )


def combine(first, second):
    peak = jnp.maximum(first[0], second[0])
    scale_first = jnp.exp(first[0] - peak)
    scale_second = jnp.exp(second[0] - peak)
    total = first[1] * scale_first + second[1] * scale_second
    output = first[2] * scale_first[..., None] + second[2] * scale_second[..., None]
    return (peak, total, output)


def body(
    merger_rows,
    out_weight,
    kv_weight,
    kv_bias,
    merge_map,
    owner_map,
    old_memory,
    queries,
    retrieved,
):
    blocks = lax.axis_size("blk")
    copies = lax.axis_size("rep")
    head_groups = lax.axis_size("head")
    tok_rows = merger_rows.shape[0]
    visual = jnp.dot(
        merger_rows,
        lax.all_gather(out_weight, "blk", axis=0, tiled=True),
        preferred_element_type=jnp.float32,
    ).astype(jnp.bfloat16)
    half_rows = tok_rows // copies
    local_heads = KVH // head_groups
    width = kv_weight.shape[1] // KVH
    head_size = width // 2
    split_rows = visual.reshape(copies, half_rows, visual.shape[1])
    kv_columns = kv_weight.reshape(kv_weight.shape[0], KVH, width)
    indices = jnp.arange(lax.axis_size(("head", "rep")) * local_heads, dtype=jnp.int32)
    within = indices % (copies * local_heads)
    heads = indices // (copies * local_heads) * local_heads + within % local_heads
    picked_rows = jnp.take(split_rows, within // local_heads, axis=0)
    picked_cols = jnp.take(kv_columns, heads, axis=1)
    keyval = lax.psum_scatter(
        jnp.einsum(
            "crd,dcf->crf", picked_rows, picked_cols, preferred_element_type=jnp.float32
        ).astype(jnp.bfloat16),
        ("head", "rep"),
        scatter_dimension=0,
        tiled=True,
    ).astype(jnp.float32)
    keyval = (keyval + kv_bias[:, None, :]).astype(jnp.bfloat16)
    keyval = jnp.transpose(keyval, (1, 0, 2))
    unit_count = half_rows // UNIT_TOK
    units = jnp.take(keyval, merge_map[0], axis=0).reshape(
        unit_count, UNIT_TOK * local_heads * width
    )
    capacity = 2 * ((unit_count + blocks - 1) // blocks)
    owners = owner_map[:, 0]
    positions = jnp.arange(unit_count, dtype=jnp.int32)
    same_owner = owners[:, None] == owners[None, :]
    earlier = positions[None, :] < positions[:, None]
    ranks = jnp.sum((same_owner & earlier).astype(jnp.int32), axis=1)
    slots = owners * capacity + ranks
    select = slots[None, :] == jnp.arange(blocks * capacity, dtype=jnp.int32)[:, None]
    send = jnp.dot(select.astype(jnp.bfloat16), units, preferred_element_type=jnp.float32).astype(
        jnp.bfloat16
    )
    send = send.reshape(blocks, capacity, UNIT_TOK, local_heads, width)
    group_index = lax.axis_index("blk") * copies + lax.axis_index("rep")
    old_count = old_memory.shape[0]
    unit_ids = old_count * blocks * copies + group_index * unit_count + positions
    send_ids = jnp.sum(jnp.where(select, unit_ids[None, :], 0), axis=1) + jnp.where(
        jnp.any(select, axis=1), 0, -1
    )
    send_ids = send_ids.reshape(blocks, capacity)
    arrived, arrived_ids = (
        lax.all_to_all(send, "blk", split_axis=0, concat_axis=0, tiled=True),
        lax.all_to_all(send_ids, "blk", split_axis=0, concat_axis=0, tiled=True),
    )
    new_memory = arrived.reshape(blocks * capacity, UNIT_TOK, local_heads, width)
    arrived_ids = arrived_ids.reshape(blocks * capacity)
    old_ids = group_index * old_count + jnp.arange(old_count, dtype=jnp.int32)
    query_rows = queries.shape[1]
    per_head = queries.shape[3] // head_size
    slice_rows = query_rows // copies
    asked = lax.all_gather(queries, "blk", axis=0, tiled=True)
    question_count = asked.shape[0]
    block_size = math.gcd(question_count, max(1, 512 // (query_rows * local_heads * per_head)))
    block_count = question_count // block_size
    asked = asked.reshape(block_count, block_size, query_rows, local_heads, per_head, head_size)
    memory = jnp.concatenate([old_memory, new_memory], axis=0)
    flat = memory.reshape(-1, local_heads, width)
    keys = flat[..., :head_size]
    values = flat[..., head_size:]
    listed = jnp.any(
        retrieved[:, :, None] == jnp.concatenate([old_ids, arrived_ids])[None, None, :], axis=1
    )
    token_mask = jnp.repeat(listed, memory.shape[1], axis=1).reshape(
        block_count, block_size, flat.shape[0]
    )

    def attend_block(pair):
        query, mask = pair
        scores = jnp.einsum(
            "aqkhd,tkd->aqkht", query, keys, preferred_element_type=jnp.float32
        ) * head_size ** (-0.5)
        wide_mask = mask[:, None, None, None, :]
        peak = jnp.max(jnp.where(wide_mask, scores, -1e30), axis=-1)
        weights = jnp.where(wide_mask, jnp.exp(scores - peak[..., None]), 0.0)
        total = jnp.sum(weights, axis=-1)
        output = jnp.einsum(
            "aqkht,tkd->aqkhd",
            weights.astype(jnp.bfloat16),
            values,
            preferred_element_type=jnp.float32,
        )
        return (peak, total, output)

    peak, total, output = lax.map(attend_block, (asked, token_mask))
    peak = peak.reshape(question_count, query_rows, local_heads, per_head)
    total = total.reshape(question_count, query_rows, local_heads, per_head)
    output = output.reshape(question_count, query_rows, local_heads, per_head, head_size)
    partial_sums = (peak, total, output)
    peak, total, output = combined_all(partial_sums, ("blk", "rep"), combine)
    result = output / total[..., None]
    result = lax.dynamic_slice_in_dim(result, lax.axis_index("blk"), 1, 0)
    result = lax.dynamic_slice_in_dim(result, lax.axis_index("rep") * slice_rows, slice_rows, 1)
    answer = result.reshape(1, slice_rows, local_heads, per_head * head_size).astype(jnp.bfloat16)
    return (answer, new_memory)


def solution(mesh):
    placed = (
        P(("groups", "blk"), None),
        P("blk", ("head", "rep")),
        P(("head", "rep"), None),
        P("head", None),
        P(("groups", "blk", "rep"), None),
        P(("groups", "blk", "rep"), None),
        P(("groups", "blk", "rep"), None, "head", None),
        P(("groups", "blk"), None, "head", None),
        P("groups", None),
    )
    return jax.shard_map(
        body,
        mesh=mesh,
        in_specs=placed,
        out_specs=(
            P(("groups", "blk"), "rep", "head", None),
            P(("groups", "blk", "rep"), None, "head", None),
        ),
        check_vma=False,
    )
```

profile of v0, /device:TPU:0, one launch (start us, length us, event | category | flops | bytes accessed | tf_op | source)
XLA Modules:
  0.0 507.0 jit_solution(16224136639342004739)
XLA Ops:
  7.2 0.0 all-gather.3.cloned.1.call-start
  7.2 0.7 all-gather.3.cloned.1.call-update
  7.9 0.0 reduce-scatter.2.cloned.1.call-start
  8.0 12.4 %copy.40 = bf16[2048,2048]{0,1:T(8,128)(2,1)} copy(bf16[2048,2048]{1,0:T(8,128)(2,1)} %param.15) | data formatting | bytes 16777216 | tf_op args[2]
  20.3 13.1 %gather_fusion.1 = bf16[16,2048,256]{1,2,0:T(8,128)(2,1)} fusion(bf16[2048,8,256]{0,2,1:T(8,128)(2,1)} %bitcast.126, s32[1024]{0:T(1024)S(1)} %pad_clamp_fusion.1), kind=kCustom, calls=%fused_computation.1 | custom fusion | bytes 33554496 | tf_op jit(solution)/shard_map/jit(_take)/gather | solution.py:66
  33.5 335.7 %all-gather.3.cloned.1.call-done = bf16[5120,2048]{1,0:T(8,128)(2,1)} async-done(((bf16[1280,2048]{1,0:T(8,128)(2,1)}), bf16[5120,2048]{1,0:T(8,128)(2,1)}) %all-gather.3.cloned.1.call-update) | async-done | bytes 20971536 | tf_op jit(solution)/shard_map/all_gather | solution.py:53
  369.2 9.3 %convolution_convert_fusion.1 = bf16[192,2048]{1,0:T(8,128)(2,1)S(1)} fusion(bf16[192,5120]{1,0:T(8,128)(2,1)S(1)} %copy-done, bf16[5120,2048]{1,0:T(8,128)(2,1)} %all-gather.3.cloned.1.call-done), kind=kOutput, calls=%fused_computation.44 | convolution fusion | flops 4026925056 | bytes 23724032 | tf_op jit(solution)/shard_map/dot_general | solution.py:51
  378.5 3.6 gather_fusion
  382.1 11.6 %fusion.32 = bf16[16,96,256]{2,1,0:T(8,128)(2,1)} fusion(bf16[16,2048,256]{1,2,0:T(8,128)(2,1)} %gather_fusion.1, pred[16]{0:T(512)(128)(4,1)S(1)} %get-tuple-element.314, bf16[16,96,2048]{2,1,0:T(8,128)(2,1)} %gather_fusion, pred[16]{0:T(512)(128)(4,1)S(1)} %get-tuple-element.315), kind=kOutput, calls=%fused_computation.47 | convolution fusion | flops 1622540288 | bytes 23855136 | tf_op jit(solution)/shard_map/crd,dcf->crf/dot_general | solution.py:68
  393.8 0.2 convert_reduce_fusion
  394.0 0.1 fusion.42
  394.1 0.1 select_reduce_fusion.1
  394.2 0.7 add.253
  394.8 3.2 all-to-all-start
  398.1 17.6 %reduce-scatter.2.cloned.1.call-done = bf16[4,96,256]{2,1,0:T(8,128)(2,1)} async-done(((bf16[16,96,256]{2,1,0:T(8,128)(2,1)}), bf16[4,96,256]{2,1,0:T(8,128)(2,1)}) %reduce-scatter.2.cloned.1.call-update) | async-done | bytes 196624 | tf_op jit(solution)/shard_map/reduce_scatter | solution.py:67
  415.8 1.0 fusion.38
  416.7 0.2 copy.42
  416.9 0.8 gather_fusion.2
  417.6 0.2 broadcast_select_fusion
  417.8 0.1 select_n.200
  418.0 0.4 convolution_convert_fusion
  418.3 1.0 reshape.330
  419.4 4.6 all-to-all-start.1
  424.0 19.8 %all_gather.18 = bf16[4,8,4,1024]{3,1,2,0:T(8,128)(2,1)S(1)} all-gather(bf16[1,8,4,1024]{3,1,2,0:T(8,128)(2,1)S(1)} %copy.39), channel_id=1, replica_groups=mesh['groups'=2,'blk'=4,'head'=2,'rep'=2] {'blk'}, dimensions={0}, use_global_device_ids=true | all-gather | bytes 327680 | tf_op jit(solution)/shard_map/all_gather | solution.py:110
  443.9 0.5 broadcast.421
  444.4 0.6 reduce.3
  445.0 0.1 reshape.326
  445.1 0.1 compare_reduce_fusion
  445.2 0.1 broadcast_in_dim.109
  445.4 0.2 reshape_reshape.3
  445.6 3.2 pad_maximum_fusion
  448.8 0.3 copy.74
  449.1 1.5 fusion.54
  450.6 4.1 while.33
  450.6 0.7 select_reduce_fusion.3
  451.3 0.6 fusion.66
  451.9 0.7 fusion.67
  452.7 0.7 select_reduce_fusion.3
  453.3 0.6 fusion.66
  454.0 0.7 fusion.67
  454.7 0.7 copy.47
  455.5 15.1 %all_gather.21 = bf16[8,4,8,4,8]{4,2,3,1,0:T(8,128)(2,1)S(1)} all-gather(bf16[1,4,8,4,8]{4,2,3,1,0:T(8,128)(2,1)S(1)} %bitcast.135), channel_id=1, replica_groups=mesh['groups'=2,'blk'=4,'head'=2,'rep'=2] {'blk','rep'}, dimensions={0}, use_global_device_ids=true | all-gather | bytes 18432 | tf_op jit(solution)/shard_map/all_gather | solution.py:14
  470.6 15.1 %all_gather.20 = bf16[8,4,8,4,8]{4,2,3,1,0:T(8,128)(2,1)S(1)} all-gather(bf16[1,4,8,4,8]{4,2,3,1,0:T(8,128)(2,1)S(1)} %bitcast.134), channel_id=1, replica_groups=mesh['groups'=2,'blk'=4,'head'=2,'rep'=2] {'blk','rep'}, dimensions={0}, use_global_device_ids=true | all-gather | bytes 18432 | tf_op jit(solution)/shard_map/all_gather | solution.py:14
  485.8 0.8 all-gather.5.cloned.1.call-done
  486.6 1.0 fusion.37
  487.6 11.3 %while.34 = (s32[]{:T(128)}, f32[4,8,4,8]{3,2,1,0:T(4,128)S(1)}, f32[4,8,4,8]{3,2,1,0:T(4,128)S(1)}, f32[4,8,4,8,128]{4,3,2,1,0:T(8,128)S(1)}, bf16[8,4,8,4,8]{4...) while((s32[]{:T(128)}, f32[4,8,4,8]{3,2,1,0:T(4,128)S(1)}, ...), condition=%wide.region_10.11_spmd, body=%wide.region_9.10_spmd.sunk | while | flops 532485 | bytes 1355919 | solution.py:22
  487.7 0.1 fusion.68
  487.8 1.5 fusion.69
  489.3 0.1 fusion.68
  489.4 1.5 fusion.69
  490.9 0.1 fusion.68
  491.0 1.5 fusion.69
  492.5 0.1 fusion.68
  492.6 1.5 fusion.69
  494.1 0.1 fusion.68
  494.2 1.5 fusion.69
  495.7 0.1 fusion.68
  495.8 1.5 fusion.69
  497.4 0.1 fusion.68
  497.5 1.5 fusion.69
  499.0 0.1 fusion.39
  499.1 0.6 convert_element_type.151
  499.7 0.7 copy.107
  500.4 0.1 copy-done.1
  (59 shorter events, 0.5 us)
Async XLA Ops:
  7.2 362.0 %copy-start = (bf16[192,5120]{1,0:T(8,128)(2,1)S(1)}, bf16[192,5120]{1,0:T(8,128)(2,1)}, u32[]{:S(2)}) copy-start(bf16[192,5120]{1,0:T(8,128)(2,1)} %param.13) | copy-start | bytes 5898244
  7.2 362.0 %all-gather.3.cloned.1.call-start = ((), (), s32[]{:S(2)}) async-start(), calls=%async_computation.3 | async-start | bytes 26214400 | tf_op jit(solution)/shard_map/all_gather | solution.py:53
  7.9 407.8 %reduce-scatter.2.cloned.1.call-start = ((), (), s32[]{:S(2)}) async-start(), calls=%async_computation.4 | async-start | bytes 983040 | tf_op jit(solution)/shard_map/reduce_scatter | solution.py:67
  382.1 11.7 %copy-start.6 = (s32[12,1]{0,1:T(1,128)S(1)}, s32[12,1]{0,1:T(1,128)}, u32[]{:S(2)}) copy-start(s32[12,1]{0,1:T(1,128)} %param.18) | copy-start | bytes 148
  382.1 16.0 %copy-start.7 = (s32[1,96]{1,0:T(1,128)S(1)}, s32[1,96]{1,0:T(1,128)}, u32[]{:S(2)}) copy-start(s32[1,96]{1,0:T(1,128)} %param.17) | copy-start | bytes 1156
  382.1 33.6 %copy-start.4 = (f32[4,256]{1,0:T(4,128)S(1)}, f32[4,256]{1,0:T(4,128)}, u32[]{:S(2)}) copy-start(f32[4,256]{1,0:T(4,128)} %param.16) | copy-start | bytes 12292
  393.7 30.3 %copy-start.3 = (bf16[1,8,4,1024]{3,2,1,0:T(4,128)(2,1)S(1)}, bf16[1,8,4,1024]{3,2,1,0:T(4,128)(2,1)}, u32[]{:S(2)}) copy-start(bf16[1,8,4,1024]{3,2,1,0:T(4,128)(2,1)} %param.20) | copy-start | bytes 196612
  394.8 24.5 %all-to-all-start = ((s32[4,1,6]{2,1,0:T(1,128)}), s32[4,1,6]{2,1,0:T(1,128)S(1)}, u32[]{:S(2)}, u32[]{:S(2)}) async-start(s32[4,1,6]{2,1,0:T(1,128)} %bitcast.16), calls=%async_computation | async-start | bytes 4096 | tf_op jit(solution)/shard_map/all_to_all | solution.py:102
  398.1 47.0 %copy-start.5 = (s32[4,32]{1,0:T(4,128)S(1)}, s32[4,32]{1,0:T(4,128)}, u32[]{:S(2)}) copy-start(s32[4,32]{1,0:T(4,128)} %param.21) | copy-start | bytes 1540
  419.4 26.2 %all-to-all-start.1 = ((bf16[4,6,8,4,256]{4,3,2,1,0:T(4,128)(2,1)}), bf16[4,6,8,4,256]{4,3,2,1,0:T(4,128)(2,1)S(1)}, u32[]{:S(2)}, u32[]{:S(2)}) async-start(bf16[4,6,8,4,256]{4,3,2,1,0:T(4,128)(2,1)} %reshape.330), calls=%async_computation.2 | async-start | bytes 786432 | tf_op jit(solution)/shard_map/all_to_all | solution.py:101
  424.0 62.6 %all-gather.5.cloned.1.call-start = ((), (), s32[]{:S(2)}) async-start(), calls=%async_computation.5 | async-start | bytes 2359296 | tf_op jit(solution)/shard_map/all_gather | solution.py:14
  450.6 1.3 copy-start.2
  452.7 1.3 copy-start.2
  498.9 1.6 copy-start.1
Sparse Core Ops, SparseCore 0:
  9.6 359.5 all-gather.2
  393.9 21.8 reduce-scatter.1
  455.6 30.9 all-gather.4
where the time goes:
time: 508 us; the launch traced here: 507 us
  waiting for transfers between devices  355 us (70%)
  blocking collectives  50 us (10%)
  local copies, waits for them, and re-layouts  37.1 us (7%)
  matrix products  24 us (5%)
  other arithmetic  18.8 us (4%)
  between operations  14 us (3%)
  starting transfers between devices  7.92 us (2%)
    all_gather x1, waiting for transfers between devices, body(): lax.all_gather(out_weight, 'blk', axis=0, tiled=True)  336 us
    all_gather x2, blocking collectives, combined_all(): lax.all_gather(part.astype(kind), axis)  30.2 us
    all_gather x1, blocking collectives, body(): asked = lax.all_gather(queries, 'blk', axis=0, tiled=True)  19.8 us
    reduce_scatter x1, waiting for transfers between devices, body(): lax.psum_scatter(jnp.einsum('crd,dcf->crf', picked_rows, picked_cols, pre...  17.6 us
    unnamed x18, local copies, waits for them, and re-layouts  13.3 us
    gather x1, local copies, waits for them, and re-layouts, body(): picked_cols = jnp.take(kv_columns, heads, axis=1)  13.1 us
    dot_general x1, matrix products, body(): jnp.einsum('crd,dcf->crf', picked_rows, picked_cols, preferred_element_ty...  11.6 us
    add x7, other arithmetic, combine(): first[2] * scale_first[..., None] + second[2] * scale_second[..., None]  10.3 us
  transfers between devices with their start and end apart: 5, of which 3 were waited for; matrix products, arithmetic and copies ran while one was open for 6% of the time, Pallas kernels for 0%

commit v1 on v0

v1 whole, which is shorter than its diff:
```python
import jax
import jax.numpy as jnp
from jax import lax
from jax.sharding import PartitionSpec as P

KVH = 8
UNIT_TOK = 8


def project(merger_rows, out_weight, kv_weight, blocks, head_groups, copies):
    rows = merger_rows.shape[0]
    depth = out_weight.shape[0]
    split = merger_rows.reshape(rows, blocks, depth).transpose(1, 0, 2)
    features = lax.all_to_all(split, "blk", split_axis=0, concat_axis=0, tiled=True)
    visual = jnp.dot(
        features.reshape(blocks * rows, depth), out_weight, preferred_element_type=jnp.float32
    ).astype(jnp.bfloat16)
    partial = jnp.dot(visual, kv_weight, preferred_element_type=jnp.float32).astype(jnp.bfloat16)
    cols = kv_weight.shape[1] // head_groups
    partial = partial.reshape(blocks, copies, rows // copies, head_groups, cols)
    partial = partial.transpose(0, 3, 1, 2, 4).reshape(-1, rows // copies, cols)
    return lax.psum_scatter(
        partial, ("blk", "head", "rep"), scatter_dimension=0, tiled=True
    ).reshape(rows // copies, cols)


def body(
    merger_rows,
    out_weight,
    kv_weight,
    kv_bias,
    merge_map,
    owner_map,
    old_memory,
    queries,
    retrieved,
):
    blocks = lax.axis_size("blk")
    copies = lax.axis_size("rep")
    head_groups = lax.axis_size("head")
    local_heads = KVH // head_groups
    width = kv_weight.shape[1] // KVH
    head_size = width // 2
    group_index = lax.axis_index("blk") * copies + lax.axis_index("rep")

    keyval = project(merger_rows, out_weight, kv_weight, blocks, head_groups, copies)
    half_rows = keyval.shape[0]
    keyval = (keyval.astype(jnp.float32) + kv_bias.reshape(1, -1)).astype(jnp.bfloat16)

    unit_count = half_rows // UNIT_TOK
    capacity = 2 * ((unit_count + blocks - 1) // blocks)
    owners = owner_map[:, 0]
    positions = jnp.arange(unit_count, dtype=jnp.int32)
    same_owner = owners[:, None] == owners[None, :]
    earlier = positions[None, :] < positions[:, None]
    ranks = jnp.sum((same_owner & earlier).astype(jnp.int32), axis=1)
    slots = owners * capacity + ranks
    row_slots = jnp.repeat(slots * UNIT_TOK, UNIT_TOK) + jnp.tile(
        jnp.arange(UNIT_TOK, dtype=jnp.int32), unit_count
    )
    placed_at = merge_map[0][:, None] == jnp.arange(half_rows, dtype=jnp.int32)[None, :]
    row_target = jnp.sum(jnp.where(placed_at, row_slots[:, None], 0), axis=0)
    slot_rows = blocks * capacity * UNIT_TOK
    select = row_target[None, :] == jnp.arange(slot_rows, dtype=jnp.int32)[:, None]
    send = jnp.dot(select.astype(jnp.bfloat16), keyval, preferred_element_type=jnp.float32)
    send = send.astype(jnp.bfloat16).reshape(blocks, capacity * UNIT_TOK, keyval.shape[1])
    arrived = lax.all_to_all(send, "blk", split_axis=0, concat_axis=0, tiled=True)
    new_memory = arrived.reshape(blocks * capacity, UNIT_TOK, local_heads, width)

    old_count = old_memory.shape[0]
    old_ids = group_index * old_count + jnp.arange(old_count, dtype=jnp.int32)
    new_ids = old_count * blocks * copies + group_index * unit_count + positions
    old_listed = jnp.any(retrieved[:, :, None] == old_ids[None, None, :], axis=1)
    new_listed = jnp.any(retrieved[:, :, None] == new_ids[None, None, :], axis=1)
    slot_listed = jnp.repeat(new_listed, UNIT_TOK, axis=1)
    row_listed = jnp.any(slot_listed[:, :, None] & placed_at[None], axis=1)
    mask = jnp.concatenate([jnp.repeat(old_listed, UNIT_TOK, axis=1), row_listed], axis=1)

    query_rows = queries.shape[1]
    per_head = queries.shape[3] // head_size
    slice_rows = query_rows // copies
    asked = lax.all_gather(queries, "blk", axis=0, tiled=True)
    questions = asked.shape[0]
    asked = asked.reshape(questions, query_rows, local_heads, per_head, head_size)
    old_flat = old_memory.reshape(-1, local_heads, width)
    flat = jnp.concatenate([old_flat, keyval.reshape(half_rows, local_heads, width)], axis=0)
    keys = flat[..., :head_size]
    values = flat[..., head_size:]
    wide_mask = mask[None, :, None, None, :]
    scores = jnp.einsum("aqkhd,tkd->kaqht", asked, keys, preferred_element_type=jnp.float32)
    scores = jnp.where(wide_mask, scores * head_size ** (-0.5), -1e30)
    peak = jnp.max(scores, axis=-1)
    weights = jnp.where(wide_mask, jnp.exp(scores - peak[..., None]), 0.0)
    total = jnp.sum(weights, axis=-1)
    output = jnp.einsum(
        "kaqht,tkd->kaqhd", weights.astype(jnp.bfloat16), values, preferred_element_type=jnp.float32
    )

    def by_holder(part):
        part = part.reshape((local_heads, questions, copies, slice_rows) + part.shape[3:])
        part = jnp.moveaxis(part, 0, 3)
        return part.reshape((questions * copies, slice_rows * local_heads * per_head) + part.shape[5:])

    answer_rows = slice_rows * local_heads * per_head
    stat_rows = -(-answer_rows // head_size)
    spare = ((0, 0), (0, stat_rows * head_size - answer_rows))
    stats = jnp.stack([jnp.pad(by_holder(peak), spare), jnp.pad(by_holder(total), spare)], axis=1)
    partial = jnp.concatenate(
        [by_holder(output), stats.reshape(questions * copies, 2 * stat_rows, head_size)], axis=1
    )
    partial = lax.all_to_all(partial, ("blk", "rep"), split_axis=0, concat_axis=0, tiled=True)
    outputs = partial[:, :answer_rows]
    stats = partial[:, answer_rows:].reshape(-1, 2, stat_rows * head_size)[..., :answer_rows]
    scale = jnp.exp(stats[:, 0] - jnp.max(stats[:, 0], axis=0, keepdims=True))
    total = jnp.sum(stats[:, 1] * scale, axis=0)
    result = jnp.sum(outputs * scale[..., None], axis=0) / total[:, None]
    answer = result.reshape(1, slice_rows, local_heads, per_head * head_size).astype(jnp.bfloat16)
    return (answer, new_memory)


def solution(mesh):
    placed = (
        P(("groups", "blk"), None),
        P("blk", ("head", "rep")),
        P(("head", "rep"), None),
        P("head", None),
        P(("groups", "blk", "rep"), None),
        P(("groups", "blk", "rep"), None),
        P(("groups", "blk", "rep"), None, "head", None),
        P(("groups", "blk"), None, "head", None),
        P("groups", None),
    )
    return jax.shard_map(
        body,
        mesh=mesh,
        in_specs=placed,
        out_specs=(
            P(("groups", "blk"), "rep", "head", None),
            P(("groups", "blk", "rep"), None, "head", None),
        ),
        check_vma=False,
    )
```

time: 508 us -> 198 us (0.39)
  waiting for transfers between devices: 355 us -> 67.5 us
  local copies, waits for them, and re-layouts: 37.1 us -> 17.1 us
  blocking collectives: 50 us -> 66.1 us
  other arithmetic: 18.8 us -> 4.13 us
    all_gather x2 -> x0, waiting for transfers between devices: 337 us -> none  [the longest x1 336 us: body(): lax.all_gather(out_weight, 'blk', axis=0, tiled=True)]
    all_to_all x0 -> x1, blocking collectives: none -> 51.5 us  [project(): lax.all_to_all(split, 'blk', split_axis=0, concat_axis=0, tiled=True)]
    all_gather x2 -> x0, blocking collectives: 30.2 us -> none  [combined_all(): lax.all_gather(part.astype(kind), axis)]
    reduce_scatter x1, waiting for transfers between devices: 17.6 us -> 46.8 us  [project(): lax.psum_scatter(partial, ('blk', 'head', 'rep'), scatter_dimension=0, ti...]
    gather x3 -> x0, local copies, waits for them, and re-layouts: 17.5 us -> none  [the longest x1 13.1 us: body(): picked_cols = jnp.take(kv_columns, heads, axis=1)]
    all_to_all x1, waiting for transfers between devices: 0.01 us -> 15 us  [body(): lax.all_to_all(partial, ('blk', 'rep'), split_axis=0, concat_axis=0, tile...]
    reshape x2 -> x6, local copies, waits for them, and re-layouts: 1.11 us -> 12.4 us  [the longest x2 7.41 us: project(): partial = partial.reshape(blocks, copies, rows // copies, head_groups, cols)]
    unnamed x18, local copies, waits for them, and re-layouts: 13.3 us -> 2.34 us
  transfers between devices with their start and end apart: 5 -> 3, of which waited for: 3 -> 3; matrix products, arithmetic and copies ran while one was open for 6% -> 5% of each run, Pallas kernels for 0% -> 0%
where the time goes in v1:
time: 198 us
  waiting for transfers between devices  67.5 us (34%)
  blocking collectives  66.1 us (33%)
  matrix products  21.5 us (11%)
  local copies, waits for them, and re-layouts  17.1 us (9%)
  between operations  14.3 us (7%)
  starting transfers between devices  7.22 us (4%)
  other arithmetic  4.13 us (2%)
    all_to_all x1, blocking collectives, project(): lax.all_to_all(split, 'blk', split_axis=0, concat_axis=0, tiled=True)  51.5 us
    reduce_scatter x1, waiting for transfers between devices, project(): lax.psum_scatter(partial, ('blk', 'head', 'rep'), scatter_dimension=0, ti...  46.8 us
    dot_general x1, matrix products, project(): jnp.dot(visual, kv_weight, preferred_element_type=jnp.float32)  17.3 us
    all_to_all x1, waiting for transfers between devices, body(): lax.all_to_all(partial, ('blk', 'rep'), split_axis=0, concat_axis=0, tile...  15 us
    all_gather x1, blocking collectives, body(): asked = lax.all_gather(queries, 'blk', axis=0, tiled=True)  14.6 us
    reshape x2, local copies, waits for them, and re-layouts, project(): partial = partial.reshape(blocks, copies, rows // copies, head_groups, cols)  7.41 us
    all_to_all x1, waiting for transfers between devices, body(): lax.all_to_all(send, 'blk', split_axis=0, concat_axis=0, tiled=True)  5.82 us
  transfers between devices with their start and end apart: 3, of which 3 were waited for; matrix products, arithmetic and copies ran while one was open for 5% of the time, Pallas kernels for 0%

profile of v1, /device:TPU:0, one launch (start us, length us, event | category | flops | bytes accessed | tf_op | source)
XLA Modules:
  0.0 197.9 jit_solution(10111951723759914340)
XLA Ops:
  7.2 0.0 reduce-scatter.2.cloned.1.call-start
  7.2 3.8 %reshape.153 = bf16[192,4,1280]{2,1,0:T(4,128)(2,1)S(1)} reshape(bf16[192,5120]{1,0:T(8,128)(2,1)} %param.9) | data formatting | bytes 3932160 | tf_op jit(solution)/shard_map/reshape | solution.py:13
  11.0 0.2 copy.44
  11.2 51.5 %all_to_all.15 = bf16[4,192,1280]{2,1,0:T(8,128)(2,1)S(1)} all-to-all(bf16[4,192,1280]{2,1,0:T(8,128)(2,1)S(1)} %copy.44), channel_id=1, replica_groups=mesh['groups'=2,'blk'=4,'head'=2,'rep'=2] {'blk'}, dimensions={0} | all-to-all | bytes 3932160 | tf_op jit(solution)/shard_map/all_to_all | solution.py:14
  62.7 17.3 %convolution_convert_fusion = bf16[768,2048]{1,0:T(8,128)(2,1)} fusion(bf16[2048,2048]{1,0:T(8,128)(2,1)} %param.11, bf16[768,1280]{1,0:T(8,128)(2,1)S(1)} %bitcast.83, bf16[1280,2048]{1,0:T(8,128)(2,1)} %param.10), kind=kOutput, calls=%fused_computation.6 | convolution fusion | flops 10472128512 | bytes 18743296 | tf_op jit(solution)/shard_map/dot_general | solution.py:18
  80.0 4.8 %reshape.155 = bf16[4,2,96,2,1024]{4,3,2,1,0:T(2,128)(2,1)S(1)} reshape(bf16[768,2048]{1,0:T(8,128)(2,1)} %convolution_convert_fusion) | data formatting | bytes 6291456 | tf_op jit(solution)/shard_map/reshape | solution.py:20
  84.8 2.7 %copy.45 = bf16[4,2,96,2,1024]{4,2,1,3,0:T(8,128)(2,1)} copy(bf16[4,2,96,2,1024]{4,3,2,1,0:T(2,128)(2,1)S(1)} %reshape.155) | data formatting | bytes 6291456 | tf_op jit(solution)/shard_map/reshape | solution.py:20
  87.4 0.0 copy-start.4
  87.4 0.0 copy-start
  87.4 0.0 copy-start.2
  87.4 0.0 reduce-scatter.2.cloned.1.call-update
  87.5 0.0 copy-start.6
  87.5 0.0 copy-start.3
  87.5 0.0 copy-start.5
  87.5 0.6 copy-done.4
  88.1 0.4 compare_reduce_fusion.1
  88.5 0.1 copy.42
  88.6 0.1 broadcast_in_dim.56
  88.7 0.1 and.20
  88.8 0.1 compare_reduce_fusion
  88.9 0.1 broadcast_in_dim.55
  89.0 0.2 reshape.151
  89.2 0.0 copy-done
  89.2 1.6 copy.68
  90.9 0.0 copy-done.2
  90.9 0.0 copy-start.1
  90.9 14.6 %all_gather.3 = bf16[4,8,4,1024]{3,1,2,0:T(8,128)(2,1)S(1)} all-gather(bf16[1,8,4,1024]{3,1,2,0:T(8,128)(2,1)S(1)} %copy.47), channel_id=1, replica_groups=mesh['groups'=2,'blk'=4,'head'=2,'rep'=2] {'blk'}, dimensions={0}, use_global_device_ids=true | all-gather | bytes 327680 | tf_op jit(solution)/shard_map/all_gather | solution.py:82
  105.5 0.0 copy-done.6
  105.5 0.2 convert_reduce_fusion
  105.7 0.1 iota_add_fusion
  105.8 0.1 add.62
  105.9 0.0 copy-done.3
  105.9 0.0 copy-done.5
  105.9 0.1 select_reduce_fusion
  106.0 0.1 iota_compare_fusion.2
  106.1 0.1 and_reduce_fusion
  106.3 46.8 %reduce-scatter.2.cloned.1.call-done = bf16[1,96,1024]{2,1,0:T(8,128)(2,1)} async-done(((bf16[16,96,1024]{2,1,0:T(8,128)(2,1)}), bf16[1,96,1024]{2,1,0:T(8,128)(2,1)}) %reduce-scatter.2.cloned.1.call-update) | async-done | bytes 196624 | tf_op jit(solution)/shard_map/reduce_scatter | solution.py:22
  153.0 1.1 reshape.164
  154.1 0.1 fusion.17
  154.2 1.9 convolution_convert_fusion.2
  156.1 3.6 %all-to-all-start.2 = ((bf16[4,48,1024]{2,1,0:T(8,128)(2,1)}), bf16[4,48,1024]{2,1,0:T(8,128)(2,1)S(1)}, u32[]{:S(2)}, u32[]{:S(2)}) async-start(bf16[4,48,1024]{2,1,0:T(8,128)(2,1)} %bitcast.23), calls=%async_computation.3 | async-start | bytes 786432 | tf_op jit(solution)/shard_map/all_to_all | solution.py:67
  159.8 0.0 copy-done.1
  159.8 1.0 fusion
  160.8 1.2 fusion.3
  162.1 0.1 copy.49
  162.1 1.3 fusion.1
  163.5 0.1 stack.7
  163.6 0.1 stack.6
  163.7 0.8 pad_maximum_fusion.1
  164.5 5.8 %all-to-all-done.2 = bf16[4,48,1024]{2,1,0:T(8,128)(2,1)S(1)} async-done(((bf16[4,48,1024]{2,1,0:T(8,128)(2,1)}), bf16[4,48,1024]{2,1,0:T(8,128)(2,1)S(1)}, u32[]{:S(2)}, u32[]{:S(2)}) %all-to-all-start.2) | async-done | bytes 393248 | tf_op jit(solution)/shard_map/all_to_all | solution.py:67
  170.3 3.5 %all-to-all-start.1 = ((f32[8,130,128]{2,1,0:T(8,128)}), f32[8,130,128]{2,1,0:T(8,128)S(1)}, u32[]{:S(2)}, u32[]{:S(2)}) async-start(f32[8,130,128]{2,1,0:T(8,128)} %pad_maximum_fusion.1), calls=%async_computation.2 | async-start | bytes 1114112 | tf_op jit(solution)/shard_map/all_to_all | solution.py:111
  173.9 1.0 reshape.163
  174.9 15.0 %all-to-all-done.1 = f32[8,130,128]{2,1,0:T(8,128)S(1)} async-done(((f32[8,130,128]{2,1,0:T(8,128)}), f32[8,130,128]{2,1,0:T(8,128)S(1)}, u32[]{:S(2)}, u32[]{:S(2)}) %all-to-all-start.1) | async-done | bytes 532512 | tf_op jit(solution)/shard_map/all_to_all | solution.py:111
  189.9 0.1 div.20
  190.0 0.1 div.21
  190.1 0.2 fusion.15
  190.4 0.6 divide_convert_fusion
  (14 shorter events, 0.3 us)
Async XLA Ops:
  7.2 145.9 %reduce-scatter.2.cloned.1.call-start = ((), (), s32[]{:S(2)}) async-start(), calls=%async_computation.4 | async-start | bytes 3342336 | tf_op jit(solution)/shard_map/reduce_scatter | solution.py:22
  87.4 0.7 copy-start.4
  87.4 1.8 copy-start
  87.4 3.4 %copy-start.2 = (bf16[1,8,4,1024]{3,2,1,0:T(4,128)(2,1)S(1)}, bf16[1,8,4,1024]{3,2,1,0:T(4,128)(2,1)}, u32[]{:S(2)}) copy-start(bf16[1,8,4,1024]{3,2,1,0:T(4,128)(2,1)} %param.16) | copy-start | bytes 196612
  87.5 18.1 %copy-start.6 = (s32[12,1]{0,1:T(1,128)S(1)}, s32[12,1]{0,1:T(1,128)}, u32[]{:S(2)}) copy-start(s32[12,1]{0,1:T(1,128)} %param.14) | copy-start | bytes 148
  87.5 18.4 %copy-start.3 = (f32[4,256]{1,0:T(4,128)S(1)}, f32[4,256]{1,0:T(4,128)}, u32[]{:S(2)}) copy-start(f32[4,256]{1,0:T(4,128)} %param.12) | copy-start | bytes 12292
  87.5 18.4 %copy-start.5 = (s32[1,96]{1,0:T(1,128)S(1)}, s32[1,96]{1,0:T(1,128)}, u32[]{:S(2)}) copy-start(s32[1,96]{1,0:T(1,128)} %param.13) | copy-start | bytes 1156
  90.9 68.9 %copy-start.1 = (bf16[128,8,4,256]{3,1,0,2:T(8,128)(2,1)S(1)}, bf16[128,8,4,256]{3,1,0,2:T(8,128)(2,1)}, u32[]{:S(2)}) copy-start(bf16[128,8,4,256]{3,1,0,2:T(8,128)(2,1)} %copy.68) | copy-start | bytes 6291460
  156.1 14.2 %all-to-all-start.2 = ((bf16[4,48,1024]{2,1,0:T(8,128)(2,1)}), bf16[4,48,1024]{2,1,0:T(8,128)(2,1)S(1)}, u32[]{:S(2)}, u32[]{:S(2)}) async-start(bf16[4,48,1024]{2,1,0:T(8,128)(2,1)} %bitcast.23), calls=%async_computation.3 | async-start | bytes 786432 | tf_op jit(solution)/shard_map/all_to_all | solution.py:67
  170.3 19.5 %all-to-all-start.1 = ((f32[8,130,128]{2,1,0:T(8,128)}), f32[8,130,128]{2,1,0:T(8,128)S(1)}, u32[]{:S(2)}, u32[]{:S(2)}) async-start(f32[8,130,128]{2,1,0:T(8,128)} %pad_maximum_fusion.1), calls=%async_computation.2 | async-start | bytes 1114112 | tf_op jit(solution)/shard_map/all_to_all | solution.py:111
Sparse Core Ops, SparseCore 0:
  87.6 65.3 reduce-scatter.1

commit v2 on v1

--- a/solution.py
+++ b/solution.py
@@ -1,6 +1,8 @@
 import jax
 import jax.numpy as jnp
 from jax import lax
+from jax.experimental import pallas as pl
+from jax.experimental.pallas import tpu as pltpu
 from jax.sharding import PartitionSpec as P
 
 KVH = 8
@@ -22,6 +24,316 @@
     return lax.psum_scatter(
         partial, ("blk", "head", "rep"), scatter_dimension=0, tiled=True
     ).reshape(rows // copies, cols)
+
+
+TILE = 512
+ORDER = (0, 2, 3, 1)
+VMEM_BYTES = 48 * 1024 * 1024
+
+
+def partner(block, k):
+    if k == 0:
+        return block
+    if k == 1:
+        return block + 1 - 2 * (block % 2)
+    if k == 2:
+        return block + 2 - 4 * (block // 2)
+    return 3 - block
+
+
+def project_kernel(
+    rows_ref,
+    weight_ref,
+    kv_ref,
+    bias_ref,
+    queries_ref,
+    keyval_ref,
+    asked_ref,
+    weight,
+    kv,
+    feats,
+    visual,
+    sums,
+    got_rep,
+    half_sums,
+    got_head,
+    own_sums,
+    got_blk,
+    got_queries,
+    local_sem,
+    feat_send,
+    feat_recv,
+    sum_send,
+    sum_recv,
+    query_send,
+    query_recv,
+):
+    block = lax.axis_index("blk")
+    head = lax.axis_index("head")
+    rep = lax.axis_index("rep")
+    rows, depth = feats.shape[1:]
+    half = rows // 2
+    quarter = rows // 4
+    cols = kv.shape[1]
+    half_cols = cols // 2
+    to_head = {"head": 1 - head}
+    to_rep = {"rep": 1 - rep}
+
+    def to_blk(k):
+        return {"blk": partner(block, k)}
+
+    def remote(src, dst, send, recv, device):
+        return pltpu.make_async_remote_copy(
+            src_ref=src,
+            dst_ref=dst,
+            send_sem=send,
+            recv_sem=recv,
+            device_id=device,
+            device_id_type=pl.DeviceIdType.MESH,
+        )
+
+    def quarter_rows(h, r):
+        return pl.ds(pl.multiple_of((h * 2 + r) * quarter, quarter), quarter)
+
+    own_rows = quarter_rows(head, rep)
+    over_head_rows = quarter_rows(1 - head, rep)
+
+    def feature_columns(k):
+        return pl.ds(pl.multiple_of(partner(block, k) * depth, depth), depth)
+
+    load_rows = pltpu.make_async_copy(
+        rows_ref.at[:, feature_columns(0)], feats.at[0], local_sem.at[0]
+    )
+    load_weight = pltpu.make_async_copy(weight_ref, weight, local_sem.at[1])
+    load_kv = pltpu.make_async_copy(kv_ref, kv, local_sem.at[2])
+    load_rows.start()
+    load_weight.start()
+    load_kv.start()
+
+    barrier = pltpu.get_barrier_semaphore()
+    for device in (to_blk(1), to_blk(2), to_blk(3), to_head, to_rep):
+        pl.semaphore_signal(
+            barrier, inc=1, device_id=device, device_id_type=pl.DeviceIdType.MESH
+        )
+    pl.semaphore_wait(barrier, 5)
+
+    started = []
+
+    def begin(copy):
+        copy.start()
+        started.append(copy)
+        return copy
+
+    over_blk = {}
+    for k in ORDER[1:]:
+        over_blk[k] = begin(
+            remote(
+                rows_ref.at[own_rows, feature_columns(k)],
+                feats.at[k, own_rows],
+                feat_send.at[0, k],
+                feat_recv.at[0, k],
+                to_blk(k),
+            )
+        )
+    asked = [
+        begin(
+            remote(
+                queries_ref, got_queries.at[k], query_send.at[k], query_recv.at[k], to_blk(k)
+            )
+        )
+        for k in (1, 2, 3)
+    ]
+
+    over_head, over_rep, last_rep = {}, {}, {}
+
+    def pass_quarter(k):
+        over_blk[k].wait_recv()
+        piece = feats.at[k, own_rows]
+        over_head[k] = begin(
+            remote(piece, piece, feat_send.at[1, k], feat_recv.at[1, k], to_head)
+        )
+        over_rep[k] = begin(
+            remote(piece, piece, feat_send.at[2, k], feat_recv.at[2, k], to_rep)
+        )
+
+    def pass_second(k):
+        over_head[k].wait_recv()
+        piece = feats.at[k, over_head_rows]
+        last_rep[k] = begin(
+            remote(piece, piece, feat_send.at[3, k], feat_recv.at[3, k], to_rep)
+        )
+
+    def have_rows(k):
+        over_rep[k].wait_recv()
+        last_rep[k].wait_recv()
+
+    def multiply(k):
+        @pl.loop(0, weight.shape[1] // TILE)
+        def _(i):
+            at = pl.ds(pl.multiple_of(i * TILE, TILE), TILE)
+            visual[:, at] = jnp.dot(
+                feats[k], weight[:, at], preferred_element_type=jnp.float32
+            ).astype(jnp.bfloat16)
+
+        if k == 0:
+            load_kv.wait()
+
+        @pl.loop(0, cols // TILE)
+        def _(i):
+            at = pl.ds(pl.multiple_of(i * TILE, TILE), TILE)
+            sums[k, :, at] = jnp.dot(
+                visual[...], kv[:, at], preferred_element_type=jnp.float32
+            ).astype(jnp.bfloat16)
+
+    own_half = pl.ds(pl.multiple_of(rep * half, half), half)
+    other_half = pl.ds(pl.multiple_of((1 - rep) * half, half), half)
+    own_cols = pl.ds(pl.multiple_of(head * half_cols, half_cols), half_cols)
+    other_cols = pl.ds(pl.multiple_of((1 - head) * half_cols, half_cols), half_cols)
+    by_rep, by_head, by_blk = {}, {}, {}
+
+    def send_rep(k):
+        by_rep[k] = begin(
+            remote(
+                sums.at[k, other_half],
+                got_rep.at[k],
+                sum_send.at[0, k],
+                sum_recv.at[0, k],
+                to_rep,
+            )
+        )
+
+    def send_head(k):
+        by_rep[k].wait_recv()
+        half_sums[k] = (
+            sums[k, own_half, :].astype(jnp.float32) + got_rep[k].astype(jnp.float32)
+        ).astype(jnp.bfloat16)
+        by_head[k] = begin(
+            remote(
+                half_sums.at[k, :, other_cols],
+                got_head.at[k],
+                sum_send.at[1, k],
+                sum_recv.at[1, k],
+                to_head,
+            )
+        )
+
+    def send_blk(k):
+        by_head[k].wait_recv()
+        own_sums[k] = (
+            half_sums[k, :, own_cols].astype(jnp.float32) + got_head[k].astype(jnp.float32)
+        ).astype(jnp.bfloat16)
+        if k != 0:
+            by_blk[k] = begin(
+                remote(
+                    own_sums.at[k],
+                    got_blk.at[k],
+                    sum_send.at[2, k],
+                    sum_recv.at[2, k],
+                    to_blk(k),
+                )
+            )
+
+    first, second, third, fourth = ORDER
+    load_rows.wait()
+    load_weight.wait()
+    multiply(first)
+    send_rep(first)
+    pass_quarter(second)
+    pass_second(second)
+    send_head(first)
+    pass_quarter(third)
+    have_rows(second)
+    multiply(second)
+    send_rep(second)
+    pass_second(third)
+    send_head(second)
+    send_blk(first)
+    pass_quarter(fourth)
+    have_rows(third)
+    multiply(third)
+    send_rep(third)
+    pass_second(fourth)
+    send_head(third)
+    send_blk(second)
+    have_rows(fourth)
+    multiply(fourth)
+    send_rep(fourth)
+    send_blk(third)
+    send_head(fourth)
+    send_blk(fourth)
+
+    asked_ref[block] = queries_ref[...]
+    for k in (1, 2, 3):
+        asked[k - 1].wait_recv()
+        asked_ref[partner(block, k)] = got_queries[k]
+    total = own_sums[0].astype(jnp.float32) + bias_ref[...]
+    for k in ORDER[1:]:
+        by_blk[k].wait_recv()
+        total = total + got_blk[k].astype(jnp.float32)
+    keyval_ref[...] = total.astype(jnp.bfloat16)
+    for copy in started:
+        copy.wait_send()
+
+
+def project_and_ask(merger_rows, out_weight, kv_weight, bias, queries):
+    rows = merger_rows.shape[0]
+    depth, inner = out_weight.shape
+    cols = kv_weight.shape[1]
+    half, half_cols = rows // 2, cols // 2
+    ask_rows, ask_cols = queries.shape
+    kept = jnp.bfloat16
+    macs = 4 * rows * inner * (depth + cols)
+    hbm = pl.BlockSpec(memory_space=pl.ANY)
+    vmem = pl.BlockSpec(memory_space=pltpu.VMEM)
+    return pl.pallas_call(
+        project_kernel,
+        out_shape=(
+            jax.ShapeDtypeStruct((half, half_cols), kept),
+            jax.ShapeDtypeStruct((4, ask_rows, ask_cols), kept),
+        ),
+        in_specs=[hbm, hbm, hbm, vmem, vmem],
+        out_specs=(vmem, vmem),
+        scratch_shapes=[
+            pltpu.VMEM((depth, inner), kept),
+            pltpu.VMEM((inner, cols), kept),
+            pltpu.VMEM((4, rows, depth), kept),
+            pltpu.VMEM((rows, inner), kept),
+            pltpu.VMEM((4, rows, cols), kept),
+            pltpu.VMEM((4, half, cols), kept),
+            pltpu.VMEM((4, half, cols), kept),
+            pltpu.VMEM((4, half, half_cols), kept),
+            pltpu.VMEM((4, half, half_cols), kept),
+            pltpu.VMEM((4, half, half_cols), kept),
+            pltpu.VMEM((4, ask_rows, ask_cols), kept),
+            pltpu.SemaphoreType.DMA((3,)),
+            pltpu.SemaphoreType.DMA((4, 4)),
+            pltpu.SemaphoreType.DMA((4, 4)),
+            pltpu.SemaphoreType.DMA((3, 4)),
+            pltpu.SemaphoreType.DMA((3, 4)),
+            pltpu.SemaphoreType.DMA((4,)),
+            pltpu.SemaphoreType.DMA((4,)),
+        ],
+        compiler_params=pltpu.CompilerParams(
+            collective_id=0, has_side_effects=True, vmem_limit_bytes=VMEM_BYTES
+        ),
+        cost_estimate=pl.CostEstimate(
+            flops=2 * macs,
+            bytes_accessed=2 * (rows * 4 * depth + depth * inner + inner * cols),
+            transcendentals=0,
+        ),
+    )(merger_rows, out_weight, kv_weight, bias, queries)
+
+
+def tiles_fit(merger_rows, out_weight, kv_weight, blocks, head_groups, copies):
+    return (
+        blocks == 4
+        and head_groups == 2
+        and copies == 2
+        and merger_rows.shape[0] % 64 == 0
+        and out_weight.shape[0] % 128 == 0
+        and out_weight.shape[1] % TILE == 0
+        and kv_weight.shape[1] % TILE == 0
+    )
 
 
 def body(
@@ -43,9 +355,21 @@
     head_size = width // 2
     group_index = lax.axis_index("blk") * copies + lax.axis_index("rep")
 
-    keyval = project(merger_rows, out_weight, kv_weight, blocks, head_groups, copies)
+    bias = kv_bias.reshape(1, -1)
+    if tiles_fit(merger_rows, out_weight, kv_weight, blocks, head_groups, copies):
+        keyval, asked = project_and_ask(
+            merger_rows,
+            out_weight,
+            kv_weight,
+            bias,
+            queries.reshape(-1, queries.shape[3]),
+        )
+        asked = asked.reshape((blocks,) + queries.shape[1:])
+    else:
+        keyval = project(merger_rows, out_weight, kv_weight, blocks, head_groups, copies)
+        keyval = (keyval.astype(jnp.float32) + bias).astype(jnp.bfloat16)
+        asked = lax.all_gather(queries, "blk", axis=0, tiled=True)
     half_rows = keyval.shape[0]
-    keyval = (keyval.astype(jnp.float32) + kv_bias.reshape(1, -1)).astype(jnp.bfloat16)
 
     unit_count = half_rows // UNIT_TOK
     capacity = 2 * ((unit_count + blocks - 1) // blocks)
@@ -79,7 +403,6 @@
     query_rows = queries.shape[1]
     per_head = queries.shape[3] // head_size
     slice_rows = query_rows // copies
-    asked = lax.all_gather(queries, "blk", axis=0, tiled=True)
     questions = asked.shape[0]
     asked = asked.reshape(questions, query_rows, local_heads, per_head, head_size)
     old_flat = old_memory.reshape(-1, local_heads, width)

time: 198 us -> 98.2 us (0.50)
  blocking collectives: 66.1 us -> 0 us
  Pallas kernels: 0 us -> 54.2 us
  waiting for transfers between devices: 67.5 us -> 21 us
  matrix products: 21.5 us -> 3.06 us
  between operations: 14.3 us -> 0.85 us
  local copies, waits for them, and re-layouts: 17.1 us -> 5.75 us
    pallas_call x0 -> x1, Pallas kernels: none -> 54.2 us  [project_and_ask(): pl.pallas_call(project_kernel, out_shape=(jax.ShapeDtypeStruct((half, hal...]
    all_to_all x1 -> x0, blocking collectives: 51.5 us -> none  [project(): lax.all_to_all(split, 'blk', split_axis=0, concat_axis=0, tiled=True)]
    reduce_scatter x1 -> x0, waiting for transfers between devices: 46.8 us -> none  [project(): lax.psum_scatter(partial, ('blk', 'head', 'rep'), scatter_dimension=0, ti...]
    dot_general x1 -> x0, matrix products: 17.3 us -> none  [project(): jnp.dot(visual, kv_weight, preferred_element_type=jnp.float32)]
    all_gather x1 -> x0, blocking collectives: 14.6 us -> none  [body(): asked = lax.all_gather(queries, 'blk', axis=0, tiled=True)]
    reshape x3 -> x2, local copies, waits for them, and re-layouts: 11.2 us -> 0.87 us  [the longest x1 0.86 us: body(): queries.reshape(-1, queries.shape[3])]
  transfers between devices with their start and end apart: 3 -> 2, of which waited for: 3 -> 2; matrix products, arithmetic and copies ran while one was open for 5% -> 7% of each run, Pallas kernels for 0% -> 0%
where the time goes in v2:
time: 98.2 us; the launch traced here: 97.7 us
  Pallas kernels  54.2 us (55%)
  waiting for transfers between devices  21 us (21%)
  starting transfers between devices  7 us (7%)
  other arithmetic  5.86 us (6%)
  local copies, waits for them, and re-layouts  5.75 us (6%)
  matrix products  3.06 us (3%)
    pallas_call x1, Pallas kernels, project_and_ask(): pl.pallas_call(project_kernel, out_shape=(jax.ShapeDtypeStruct((half, hal...  54.2 us
    all_to_all x1, waiting for transfers between devices, body(): lax.all_to_all(partial, ('blk', 'rep'), split_axis=0, concat_axis=0, tile...  15 us
    all_to_all x1, waiting for transfers between devices, body(): lax.all_to_all(send, 'blk', split_axis=0, concat_axis=0, tiled=True)  6.04 us
    all_to_all x1, starting transfers between devices, body(): lax.all_to_all(partial, ('blk', 'rep'), split_axis=0, concat_axis=0, tile...  3.54 us
    all_to_all x1, starting transfers between devices, body(): lax.all_to_all(send, 'blk', split_axis=0, concat_axis=0, tiled=True)  3.46 us
    unnamed x11, local copies, waits for them, and re-layouts  2.56 us
  transfers between devices with their start and end apart: 2, of which 2 were waited for; matrix products, arithmetic and copies ran while one was open for 7% of the time, Pallas kernels for 0%

profile of v2, /device:TPU:0, one launch (start us, length us, event | category | flops | bytes accessed | tf_op | source)
XLA Modules:
  0.0 97.7 jit_solution(497317658747020996)
XLA Ops:
  0.6 0.9 reshape.133.queries_ref
  1.5 0.7 copy.43
  2.2 0.9 convert_reduce_fusion
  3.1 0.7 add_multiply_fusion
  3.8 0.1 iota_add_fusion
  3.8 0.1 add.43
  3.9 0.8 select_reduce_fusion
  4.7 0.0 copy-start
  4.7 1.5 %copy-done = bf16[192,5120]{1,0:T(8,128)(2,1)S(1)} copy-done((bf16[192,5120]{1,0:T(8,128)(2,1)S(1)}, bf16[192,5120]{1,0:T(8,128)(2,1)}, u32[]{:S(2)}) %copy-start) | copy-done | bytes 1966104
  6.2 0.0 copy-start.3
  6.2 0.0 copy-start.2
  6.2 0.0 copy-start.1
  6.2 54.2 %shard_map.104 = (bf16[96,1024]{1,0:T(8,128)(2,1)S(1)}, bf16[4,32,1024]{2,1,0:T(8,128)(2,1)S(1)}) custom-call(bf16[192,5120]{1,0:T(8,128)(2,1)S(1)} %copy-done, bf16[1280,2048]{1,0:T(8,128)(2,1)} %weight_ref.1, bf16[2048,2048]{1,0:T(8,128)(2,1)} %kv_ref.1, f32[1,1024]{1,0:T(1,128)S(1)} %bitcast.50, bf16[32,1024]{1,0:T(8,128)(2,1)S(1)} %reshape.133.queries_ref), custom_call_target="tpu_custom_call" | custom-call | flops 10468982784 | bytes 15597568 | tf_op jit(solution)/shard_map/pallas_call | solution.py:288
  60.5 1.0 %convolution_convert_fusion = bf16[192,1024]{1,0:T(8,128)(2,1)} fusion(bf16[96,1024]{1,0:T(8,128)(2,1)S(1)} %get-tuple-element.5, s32[96]{0:T(128)S(1)} %select_reduce_fusion), kind=kOutput, calls=%fused_computation.12 | convolution fusion | flops 37963776 | bytes 590208 | tf_op jit(solution)/shard_map/dot_general | solution.py:389
  61.5 3.5 %all-to-all-start.1 = ((bf16[4,48,1024]{2,1,0:T(8,128)(2,1)}), bf16[4,48,1024]{2,1,0:T(8,128)(2,1)S(1)}, u32[]{:S(2)}, u32[]{:S(2)}) async-start(bf16[4,48,1024]{2,1,0:T(8,128)(2,1)} %bitcast.17), calls=%async_computation.1 | async-start | bytes 786432 | tf_op jit(solution)/shard_map/all_to_all | solution.py:391
  65.0 0.0 copy-done.3
  65.0 0.1 iota_compare_fusion.2
  65.1 0.0 copy-done.2
  65.1 0.4 compare_reduce_fusion.1
  65.4 0.1 copy.30
  65.5 0.1 broadcast_in_dim.56
  65.6 0.1 and.20
  65.7 0.1 compare_reduce_fusion
  65.8 0.1 broadcast_in_dim.55
  66.0 0.2 reshape.131
  66.2 0.0 copy-done.1
  66.2 0.3 copy.51
  66.5 0.1 and_reduce_fusion
  66.7 1.0 %fusion.22 = (f32[4,4,8,8]{3,2,1,0:T(8,128)S(1)}, f32[4,4,8,8,1120]{4,3,2,1,0:T(8,128)S(1)}) fusion(bf16[1024,4,256]{2,0,1:T(8,128)(2,1)S(1)} %bitcast.51, bf16[96,4,256]{2,0,1:T(8,128)(2,1)S(1)} %bitcast.58, bf16[4,8,4,8,128]{4,3,2,1,0:T(8,128)(2,1)S(1)} %bitcast.56, pred[4,1120]{1,0:T(4,128)(4,1)S(1)} %pad_add_fusion), kind=kOutput, calls=%fused_computation.45 | convolution fusion | flops 299334656 | bytes 7152000 | tf_op jit(solution)/shard_map/aqkhd,tkd->kaqht/dot_general | solution.py:413
  67.7 1.0 %fusion.3 = f32[4,4,8,8,128]{4,3,2,1,0:T(8,128)S(1)} fusion(f32[4,4,8,8,1120]{4,3,2,1,0:T(8,128)S(1)} %get-tuple-element.11, f32[4,4,8,8]{3,2,1,0:T(8,128)S(1)} %get-tuple-element.10, pred[4,1120]{1,0:T(4,128)(4,1)S(1)} %pad_add_fusion, bf16[96,4,256]{2,0,1:T(8,128)(2,1)S(1)} %bitcast.59, bf16[1024,4,256]{2,0,1:T(8,128)(2,1)S(1)} %bitcast.52), kind=kOutput, calls=%fused_computation.5 | convolution fusion | flops 299335680 | bytes 7414144 | tf_op jit(solution)/shard_map/kaqht,tkd->kaqhd/dot_general | solution.py:418
  68.8 0.1 copy.34
  68.9 1.0 %fusion.1 = f32[4,4,8,8]{3,2,1,0:T(8,128)S(1)} fusion(f32[4,4,8,8,1120]{4,3,2,1,0:T(8,128)S(1)} %get-tuple-element.11, f32[4,4,8,8]{3,2,1,0:T(8,128)S(1)} %get-tuple-element.10, pred[4,1120]{1,0:T(4,128)(4,1)S(1)} %pad_add_fusion), kind=kLoop, calls=%fused_computation.3 | loop fusion | flops 3439616 | bytes 4600192 | tf_op jit(solution)/shard_map/reduce_sum | solution.py:417
  70.0 0.1 stack.7
  70.1 0.1 stack.6
  70.2 0.8 pad_maximum_fusion.1
  71.0 6.0 %all-to-all-done.1 = bf16[4,48,1024]{2,1,0:T(8,128)(2,1)S(1)} async-done(((bf16[4,48,1024]{2,1,0:T(8,128)(2,1)}), bf16[4,48,1024]{2,1,0:T(8,128)(2,1)S(1)}, u32[]{:S(2)}, u32[]{:S(2)}) %all-to-all-start.1) | async-done | bytes 393248 | tf_op jit(solution)/shard_map/all_to_all | solution.py:391
  77.1 3.5 %all-to-all-start = ((f32[8,130,128]{2,1,0:T(8,128)}), f32[8,130,128]{2,1,0:T(8,128)S(1)}, u32[]{:S(2)}, u32[]{:S(2)}) async-start(f32[8,130,128]{2,1,0:T(8,128)} %pad_maximum_fusion.1), calls=%async_computation | async-start | bytes 1114112 | tf_op jit(solution)/shard_map/all_to_all | solution.py:434
  80.6 1.0 %reshape.141 = bf16[24,8,4,256]{3,2,1,0:T(4,128)(2,1)} reshape(bf16[4,48,1024]{2,1,0:T(8,128)(2,1)S(1)} %all-to-all-done.1) | data formatting | bytes 786432 | tf_op jit(solution)/shard_map/reshape | solution.py:392
  81.6 15.0 %all-to-all-done = f32[8,130,128]{2,1,0:T(8,128)S(1)} async-done(((f32[8,130,128]{2,1,0:T(8,128)}), f32[8,130,128]{2,1,0:T(8,128)S(1)}, u32[]{:S(2)}, u32[]{:S(2)}) %all-to-all-start) | async-done | bytes 532512 | tf_op jit(solution)/shard_map/all_to_all | solution.py:434
  96.6 0.1 div.20
  96.7 0.1 div.21
  96.9 0.2 fusion.14
  97.1 0.6 divide_convert_fusion
  (12 shorter events, 0.3 us)
Async XLA Ops:
  4.7 1.6 %copy-start = (bf16[192,5120]{1,0:T(8,128)(2,1)S(1)}, bf16[192,5120]{1,0:T(8,128)(2,1)}, u32[]{:S(2)}) copy-start(bf16[192,5120]{1,0:T(8,128)(2,1)} %rows_ref.1) | copy-start | bytes 5898244
  6.2 58.7 %copy-start.3 = (s32[1,96]{1,0:T(1,128)S(1)}, s32[1,96]{1,0:T(1,128)}, u32[]{:S(2)}) copy-start(s32[1,96]{1,0:T(1,128)} %param.13) | copy-start | bytes 1156
  6.2 58.8 %copy-start.2 = (s32[4,32]{1,0:T(4,128)S(1)}, s32[4,32]{1,0:T(4,128)}, u32[]{:S(2)}) copy-start(s32[4,32]{1,0:T(4,128)} %param.17) | copy-start | bytes 1540
  6.2 60.0 %copy-start.1 = (bf16[128,8,4,256]{3,2,1,0:T(4,128)(2,1)S(1)}, bf16[128,8,4,256]{3,2,1,0:T(4,128)(2,1)}, u32[]{:S(2)}) copy-start(bf16[128,8,4,256]{3,2,1,0:T(4,128)(2,1)} %param.15) | copy-start | bytes 6291460
  61.5 15.6 %all-to-all-start.1 = ((bf16[4,48,1024]{2,1,0:T(8,128)(2,1)}), bf16[4,48,1024]{2,1,0:T(8,128)(2,1)S(1)}, u32[]{:S(2)}, u32[]{:S(2)}) async-start(bf16[4,48,1024]{2,1,0:T(8,128)(2,1)} %bitcast.17), calls=%async_computation.1 | async-start | bytes 786432 | tf_op jit(solution)/shard_map/all_to_all | solution.py:391
  77.1 19.5 %all-to-all-start = ((f32[8,130,128]{2,1,0:T(8,128)}), f32[8,130,128]{2,1,0:T(8,128)S(1)}, u32[]{:S(2)}, u32[]{:S(2)}) async-start(f32[8,130,128]{2,1,0:T(8,128)} %pad_maximum_fusion.1), calls=%async_computation | async-start | bytes 1114112 | tf_op jit(solution)/shard_map/all_to_all | solution.py:434

commit v3 on v2

--- a/solution.py
+++ b/solution.py
@@ -47,8 +47,12 @@
     kv_ref,
     bias_ref,
     queries_ref,
-    keyval_ref,
-    asked_ref,
+    stored_ref,
+    retrieved_ref,
+    merge_ref,
+    owner_ref,
+    answer_ref,
+    memory_ref,
     weight,
     kv,
     feats,
@@ -59,7 +63,23 @@
     got_head,
     own_sums,
     got_blk,
-    got_queries,
+    asked,
+    stored,
+    old_out,
+    old_out_send,
+    old_out_got,
+    old_log,
+    old_log_send,
+    old_log_got,
+    new_rows,
+    new_mask,
+    units,
+    got_units,
+    out_send,
+    out_got,
+    log_full,
+    log_send,
+    log_got,
     local_sem,
     feat_send,
     feat_recv,
@@ -67,6 +87,10 @@
     sum_recv,
     query_send,
     query_recv,
+    rep_send,
+    rep_recv,
+    end_send,
+    end_recv,
 ):
     block = lax.axis_index("blk")
     head = lax.axis_index("head")
@@ -109,6 +133,8 @@
     load_rows.start()
     load_weight.start()
     load_kv.start()
+    load_stored = pltpu.make_async_copy(stored_ref, stored, local_sem.at[3])
+    load_stored.start()
 
     barrier = pltpu.get_barrier_semaphore()
     for device in (to_blk(1), to_blk(2), to_blk(3), to_head, to_rep):
@@ -124,6 +150,12 @@
         started.append(copy)
         return copy
 
+    asking = [
+        begin(
+            remote(queries_ref, asked.at[k], query_send.at[k], query_recv.at[k], to_blk(k))
+        )
+        for k in (1, 2, 3)
+    ]
     over_blk = {}
     for k in ORDER[1:]:
         over_blk[k] = begin(
@@ -135,14 +167,6 @@
                 to_blk(k),
             )
         )
-    asked = [
-        begin(
-            remote(
-                queries_ref, got_queries.at[k], query_send.at[k], query_recv.at[k], to_blk(k)
-            )
-        )
-        for k in (1, 2, 3)
-    ]
 
     over_head, over_rep, last_rep = {}, {}, {}
 
@@ -233,6 +257,177 @@
                 )
             )
 
+    heads = stored.shape[0]
+    stored_rows = stored.shape[1]
+    head_size = asked.shape[3]
+    ask_rows = asked.shape[2] // heads
+    group = asked.shape[2]
+    new_count = half // UNIT_TOK
+    scale = head_size ** (-0.5)
+    place = block * 2 + rep
+    floats = jnp.float32
+
+    def iota(shape, dim):
+        return lax.broadcasted_iota(jnp.int32, shape, dim)
+
+    def listed(ids):
+        units_of = jnp.concatenate(
+            [retrieved_ref[pl.ds(partner(block, k), 1), :] for k in range(4)], axis=0
+        )
+        hit = jnp.zeros((4, ids.shape[1]), floats)
+        for j in range(units_of.shape[1]):
+            hit = jnp.where(ids == units_of[:, j : j + 1], 1.0, hit)
+        return hit
+
+    def row_mask(mask, count):
+        return jnp.concatenate(
+            [
+                jnp.broadcast_to(mask[k : k + 1], (count, mask.shape[1]))
+                for k in range(4)
+            ],
+            axis=0,
+        )
+
+    def flat_log(wide):
+        return jnp.transpose(wide)[:8]
+
+    def wide_log(flat):
+        return jnp.transpose(jnp.broadcast_to(flat[:1], (group, group)))
+
+    def prepare():
+        eye = iota((new_count, new_count), 0) == iota((new_count, new_count), 1)
+        owner = owner_ref[...].astype(floats)
+        owner_row = jnp.sum(jnp.where(eye, owner, 0.0), axis=0, keepdims=True)
+        earlier = iota((new_count, new_count), 1) < iota((new_count, new_count), 0)
+        rank = jnp.sum(
+            jnp.where((owner == owner_row) & earlier, 1.0, 0.0), axis=1, keepdims=True
+        )
+        capacity = units.shape[1] // UNIT_TOK
+        slot = owner * capacity + rank
+        slot_row = jnp.sum(jnp.where(eye, slot, 0.0), axis=0, keepdims=True)
+        of_unit = iota((half, new_count), 0) // UNIT_TOK == iota((half, new_count), 1)
+        slot_of = jnp.sum(jnp.where(of_unit, slot_row, 0.0), axis=1, keepdims=True)
+        position = iota((half, 1), 0)
+        target = slot_of * UNIT_TOK + (position % UNIT_TOK).astype(floats)
+        fills = merge_ref[...] == iota((half, half), 1)
+        target_row = jnp.sum(jnp.where(fills, target, 0.0), axis=0, keepdims=True)
+        unit_of = (position // UNIT_TOK).astype(floats)
+        unit_row = jnp.sum(jnp.where(fills, unit_of, 0.0), axis=0, keepdims=True)
+        slots = units.shape[0] * units.shape[1]
+        select = jnp.where(
+            iota((slots, half), 0) == target_row.astype(jnp.int32), 1.0, 0.0
+        ).astype(jnp.bfloat16)
+        base = stored_rows // UNIT_TOK * 8 + place * new_count
+        new_mask[0] = jnp.zeros(new_mask.shape[1:], floats)
+        new_mask[0, 0:4, 0:half] = listed(base + unit_row.astype(jnp.int32))
+        return select
+
+    def attend_stored():
+        ids = place * (stored_rows // UNIT_TOK) + iota((1, stored_rows), 1) // UNIT_TOK
+        mask = row_mask(listed(ids), 2 * ask_rows) > 0.0
+
+        @pl.loop(0, heads)
+        def _(h):
+            at = pl.ds(pl.multiple_of(h * ask_rows, ask_rows), ask_rows)
+            query = jnp.concatenate(
+                [asked[k, r, at, :] for k in range(4) for r in range(2)], axis=0
+            )
+            scores = lax.dot_general(
+                query,
+                stored[h, :, :head_size],
+                (((1,), (1,)), ((), ())),
+                preferred_element_type=floats,
+            )
+            scores = jnp.where(mask, scores * scale, -1e30)
+            peak = jnp.max(scores, axis=1, keepdims=True)
+            weights = jnp.where(mask, jnp.exp(scores - peak), 0.0)
+            total = jnp.maximum(jnp.sum(weights, axis=1, keepdims=True), 1e-30)
+            output = jnp.dot(
+                weights.astype(jnp.bfloat16),
+                stored[h, :, head_size:],
+                preferred_element_type=floats,
+            )
+            output = output / total
+            logs = jnp.broadcast_to(peak + jnp.log(total), output.shape)
+            for k in range(4):
+                for r in range(2):
+                    start = (2 * k + r) * ask_rows
+                    old_out[r, k, at, :] = output[start : start + ask_rows]
+                    old_log[r, k, at, :] = logs[start : start + ask_rows]
+
+        old_out_send[...] = old_out[1 - rep].astype(jnp.bfloat16)
+        for k in range(4):
+            old_log_send[k] = flat_log(old_log[1 - rep, k])
+
+    old_parts = []
+
+    def send_stored():
+        for i, (src, dst) in enumerate(
+            (
+                (old_out_send, old_out_got),
+                (old_log_send, old_log_got),
+                (new_mask.at[0], new_mask.at[1]),
+            )
+        ):
+            old_parts.append(
+                begin(remote(src, dst, rep_send.at[i], rep_recv.at[i], to_rep))
+            )
+
+    def merge_stored():
+        for copy in old_parts:
+            copy.wait_recv()
+        for k in range(4):
+            mine, theirs = old_log[rep, k], wide_log(old_log_got[k])
+            peak = jnp.maximum(mine, theirs)
+            first_part, second_part = jnp.exp(mine - peak), jnp.exp(theirs - peak)
+            total = first_part + second_part
+            old_out[rep, k] = (
+                first_part * old_out[rep, k] + second_part * old_out_got[k].astype(floats)
+            ) / total
+            old_log[rep, k] = peak + jnp.log(total)
+
+    def attend_new():
+        masks = [row_mask(new_mask[i, 0:4, 0:half], ask_rows) > 0.0 for i in range(2)]
+
+        @pl.loop(0, heads)
+        def _(h):
+            at = pl.ds(pl.multiple_of(h * ask_rows, ask_rows), ask_rows)
+            key_at = pl.ds(pl.multiple_of(h * 2 * head_size, head_size), head_size)
+            value_at = pl.ds(
+                pl.multiple_of(h * 2 * head_size + head_size, head_size), head_size
+            )
+            query = jnp.concatenate([asked[k, rep, at, :] for k in range(4)], axis=0)
+            before = jnp.concatenate([old_log[rep, k, at, :] for k in range(4)], axis=0)
+            output = jnp.concatenate([old_out[rep, k, at, :] for k in range(4)], axis=0)
+            peak, scores = before, []
+            for i in range(2):
+                part = lax.dot_general(
+                    query,
+                    new_rows[i, :, key_at],
+                    (((1,), (1,)), ((), ())),
+                    preferred_element_type=floats,
+                )
+                part = jnp.where(masks[i], part * scale, -1e30)
+                scores.append(part)
+                peak = jnp.maximum(peak, jnp.max(part, axis=1, keepdims=True))
+            total = jnp.exp(before - peak)
+            output = output * total
+            for i in range(2):
+                weights = jnp.where(masks[i], jnp.exp(scores[i] - peak[:, :half]), 0.0)
+                total = total + jnp.sum(weights, axis=1, keepdims=True)
+                output = output + jnp.dot(
+                    weights.astype(jnp.bfloat16),
+                    new_rows[i, :, value_at],
+                    preferred_element_type=floats,
+                )
+            total = jnp.maximum(total, 1e-30)
+            output = output / total
+            logs = peak + jnp.log(total)
+            for k in range(4):
+                part = slice(k * ask_rows, (k + 1) * ask_rows)
+                out_send[k, at, :] = output[part].astype(jnp.bfloat16)
+                log_full[k, at, :] = logs[part]
+
     first, second, third, fourth = ORDER
     load_rows.wait()
     load_weight.wait()
@@ -240,8 +435,15 @@
     send_rep(first)
     pass_quarter(second)
     pass_second(second)
+    select = prepare()
+    asked[0] = queries_ref[...]
+    for copy in asking:
+        copy.wait_recv()
+    load_stored.wait()
     send_head(first)
     pass_quarter(third)
+    attend_stored()
+    send_stored()
     have_rows(second)
     multiply(second)
     send_rep(second)
@@ -260,59 +462,135 @@
     send_rep(fourth)
     send_blk(third)
     send_head(fourth)
+    merge_stored()
     send_blk(fourth)
 
-    asked_ref[block] = queries_ref[...]
-    for k in (1, 2, 3):
-        asked[k - 1].wait_recv()
-        asked_ref[partner(block, k)] = got_queries[k]
-    total = own_sums[0].astype(jnp.float32) + bias_ref[...]
+    total = own_sums[0].astype(floats) + bias_ref[...]
     for k in ORDER[1:]:
         by_blk[k].wait_recv()
-        total = total + got_blk[k].astype(jnp.float32)
-    keyval_ref[...] = total.astype(jnp.bfloat16)
+        total = total + got_blk[k].astype(floats)
+    new_rows[0] = total.astype(jnp.bfloat16)
+    share = begin(
+        remote(new_rows.at[0], new_rows.at[1], rep_send.at[3], rep_recv.at[3], to_rep)
+    )
+    units[...] = (
+        jnp.dot(select, new_rows[0], preferred_element_type=floats)
+        .astype(jnp.bfloat16)
+        .reshape(units.shape)
+    )
+    share.wait_recv()
+    attend_new()
+    ended = []
+    for k in ORDER[1:]:
+        log_send[k] = flat_log(log_full[k])
+        ended.append(
+            (
+                begin(
+                    remote(
+                        out_send.at[k],
+                        out_got.at[k],
+                        end_send.at[0, k],
+                        end_recv.at[0, k],
+                        to_blk(k),
+                    )
+                ),
+                begin(
+                    remote(
+                        log_send.at[k],
+                        log_got.at[k],
+                        end_send.at[1, k],
+                        end_recv.at[1, k],
+                        to_blk(k),
+                    )
+                ),
+            )
+        )
+    relayout = []
+    for k in ORDER[1:]:
+        relayout.append(
+            begin(
+                remote(
+                    units.at[partner(block, k)],
+                    got_units.at[k],
+                    end_send.at[2, k],
+                    end_recv.at[2, k],
+                    to_blk(k),
+                )
+            )
+        )
+    memory_ref[block] = units[block]
+    logs = [log_full[0]]
+    outputs = [out_send[0].astype(floats)]
+    for k, copies in zip(ORDER[1:], ended):
+        for copy in copies:
+            copy.wait_recv()
+        logs.append(wide_log(log_got[k]))
+        outputs.append(out_got[k].astype(floats))
+    peak = jnp.maximum(jnp.maximum(logs[0], logs[1]), jnp.maximum(logs[2], logs[3]))
+    parts = [jnp.exp(one - peak) for one in logs]
+    mixed = sum(part * output for part, output in zip(parts, outputs))
+    answer_ref[...] = (mixed / sum(parts)).astype(jnp.bfloat16)
+    for k, copy in zip(ORDER[1:], relayout):
+        copy.wait_recv()
+        memory_ref[partner(block, k)] = got_units[k]
     for copy in started:
         copy.wait_send()
 
 
-def project_and_ask(merger_rows, out_weight, kv_weight, bias, queries):
+def whole_step(
+    merger_rows, out_weight, kv_weight, bias, queries, stored, retrieved, merge_map, owner_map
+):
     rows = merger_rows.shape[0]
     depth, inner = out_weight.shape
     cols = kv_weight.shape[1]
     half, half_cols = rows // 2, cols // 2
-    ask_rows, ask_cols = queries.shape
-    kept = jnp.bfloat16
+    group, head_size = queries.shape[1:]
+    new_count = half // UNIT_TOK
+    slot_rows = 2 * ((new_count + 3) // 4) * UNIT_TOK
+    kept, wide = jnp.bfloat16, jnp.float32
     macs = 4 * rows * inner * (depth + cols)
     hbm = pl.BlockSpec(memory_space=pl.ANY)
     vmem = pl.BlockSpec(memory_space=pltpu.VMEM)
+    scratch = [
+        ((depth, inner), kept),
+        ((inner, cols), kept),
+        ((4, rows, depth), kept),
+        ((rows, inner), kept),
+        ((4, rows, cols), kept),
+        ((4, half, cols), kept),
+        ((4, half, cols), kept),
+        ((4, half, half_cols), kept),
+        ((4, half, half_cols), kept),
+        ((4, half, half_cols), kept),
+        ((4, 2, group, head_size), kept),
+        (stored.shape, kept),
+        ((2, 4, group, head_size), wide),
+        ((4, group, head_size), kept),
+        ((4, group, head_size), kept),
+        ((2, 4, group, head_size), wide),
+        ((4, 8, head_size), wide),
+        ((4, 8, head_size), wide),
+        ((2, half, half_cols), kept),
+        ((2, 8, 128), wide),
+        ((4, slot_rows, half_cols), kept),
+        ((4, slot_rows, half_cols), kept),
+        ((4, group, head_size), kept),
+        ((4, group, head_size), kept),
+        ((4, group, head_size), wide),
+        ((4, 8, head_size), wide),
+        ((4, 8, head_size), wide),
+    ]
+    semaphores = [(4,), (4, 4), (4, 4), (3, 4), (3, 4), (4,), (4,), (4,), (4,), (3, 4), (3, 4)]
     return pl.pallas_call(
         project_kernel,
         out_shape=(
-            jax.ShapeDtypeStruct((half, half_cols), kept),
-            jax.ShapeDtypeStruct((4, ask_rows, ask_cols), kept),
+            jax.ShapeDtypeStruct((group, head_size), kept),
+            jax.ShapeDtypeStruct((4, slot_rows, half_cols), kept),
         ),
-        in_specs=[hbm, hbm, hbm, vmem, vmem],
+        in_specs=[hbm, hbm, hbm, vmem, vmem, hbm, vmem, vmem, vmem],
         out_specs=(vmem, vmem),
-        scratch_shapes=[
-            pltpu.VMEM((depth, inner), kept),
-            pltpu.VMEM((inner, cols), kept),
-            pltpu.VMEM((4, rows, depth), kept),
-            pltpu.VMEM((rows, inner), kept),
-            pltpu.VMEM((4, rows, cols), kept),
-            pltpu.VMEM((4, half, cols), kept),
-            pltpu.VMEM((4, half, cols), kept),
-            pltpu.VMEM((4, half, half_cols), kept),
-            pltpu.VMEM((4, half, half_cols), kept),
-            pltpu.VMEM((4, half, half_cols), kept),
-            pltpu.VMEM((4, ask_rows, ask_cols), kept),
-            pltpu.SemaphoreType.DMA((3,)),
-            pltpu.SemaphoreType.DMA((4, 4)),
-            pltpu.SemaphoreType.DMA((4, 4)),
-            pltpu.SemaphoreType.DMA((3, 4)),
-            pltpu.SemaphoreType.DMA((3, 4)),
-            pltpu.SemaphoreType.DMA((4,)),
-            pltpu.SemaphoreType.DMA((4,)),
-        ],
+        scratch_shapes=[pltpu.VMEM(shape, kind) for shape, kind in scratch]
+        + [pltpu.SemaphoreType.DMA(shape) for shape in semaphores],
         compiler_params=pltpu.CompilerParams(
             collective_id=0, has_side_effects=True, vmem_limit_bytes=VMEM_BYTES
         ),
@@ -321,10 +599,12 @@
             bytes_accessed=2 * (rows * 4 * depth + depth * inner + inner * cols),
             transcendentals=0,
         ),
-    )(merger_rows, out_weight, kv_weight, bias, queries)
-
-
-def tiles_fit(merger_rows, out_weight, kv_weight, blocks, head_groups, copies):
+    )(merger_rows, out_weight, kv_weight, bias, queries, stored, retrieved, merge_map, owner_map)
+
+
+def tiles_fit(
+    merger_rows, out_weight, kv_weight, blocks, head_groups, copies, answer_rows, head_size
+):
     return (
         blocks == 4
         and head_groups == 2
@@ -333,6 +613,8 @@
         and out_weight.shape[0] % 128 == 0
         and out_weight.shape[1] % TILE == 0
         and kv_weight.shape[1] % TILE == 0
+        and answer_rows == head_size == 128
+        and merger_rows.shape[0] // copies <= 128
     )
 
 
@@ -356,19 +638,35 @@
     group_index = lax.axis_index("blk") * copies + lax.axis_index("rep")
 
     bias = kv_bias.reshape(1, -1)
-    if tiles_fit(merger_rows, out_weight, kv_weight, blocks, head_groups, copies):
-        keyval, asked = project_and_ask(
+    query_rows = queries.shape[1]
+    per_head = queries.shape[3] // head_size
+    slice_rows = query_rows // copies
+    answer_rows = slice_rows * local_heads * per_head
+    if tiles_fit(
+        merger_rows, out_weight, kv_weight, blocks, head_groups, copies, answer_rows, head_size
+    ):
+        asking = queries.reshape(copies, slice_rows, local_heads, per_head, head_size)
+        asking = asking.transpose(0, 2, 1, 3, 4).reshape(copies, answer_rows, head_size)
+        stored = old_memory.reshape(-1, local_heads, width).transpose(1, 0, 2)
+        answer, new_memory = whole_step(
             merger_rows,
             out_weight,
             kv_weight,
             bias,
-            queries.reshape(-1, queries.shape[3]),
-        )
-        asked = asked.reshape((blocks,) + queries.shape[1:])
-    else:
-        keyval = project(merger_rows, out_weight, kv_weight, blocks, head_groups, copies)
-        keyval = (keyval.astype(jnp.float32) + bias).astype(jnp.bfloat16)
-        asked = lax.all_gather(queries, "blk", axis=0, tiled=True)
+            asking,
+            stored,
+            retrieved,
+            merge_map.reshape(-1, 1),
+            owner_map,
+        )
+        answer = answer.reshape(local_heads, slice_rows, per_head * head_size)
+        return (
+            answer.transpose(1, 0, 2)[None],
+            new_memory.reshape(-1, UNIT_TOK, local_heads, width),
+        )
+    keyval = project(merger_rows, out_weight, kv_weight, blocks, head_groups, copies)
+    keyval = (keyval.astype(jnp.float32) + bias).astype(jnp.bfloat16)
+    asked = lax.all_gather(queries, "blk", axis=0, tiled=True)
     half_rows = keyval.shape[0]
 
     unit_count = half_rows // UNIT_TOK
@@ -400,9 +698,6 @@
     row_listed = jnp.any(slot_listed[:, :, None] & placed_at[None], axis=1)
     mask = jnp.concatenate([jnp.repeat(old_listed, UNIT_TOK, axis=1), row_listed], axis=1)
 
-    query_rows = queries.shape[1]
-    per_head = queries.shape[3] // head_size
-    slice_rows = query_rows // copies
     questions = asked.shape[0]
     asked = asked.reshape(questions, query_rows, local_heads, per_head, head_size)
     old_flat = old_memory.reshape(-1, local_heads, width)
@@ -424,7 +719,6 @@
         part = jnp.moveaxis(part, 0, 3)
         return part.reshape((questions * copies, slice_rows * local_heads * per_head) + part.shape[5:])
 
-    answer_rows = slice_rows * local_heads * per_head
     stat_rows = -(-answer_rows // head_size)
     spare = ((0, 0), (0, stat_rows * head_size - answer_rows))
     stats = jnp.stack([jnp.pad(by_holder(peak), spare), jnp.pad(by_holder(total), spare)], axis=1)

time: 98.2 us -> 85.1 us (0.87)
  Pallas kernels: 54.2 us -> 77.4 us
  waiting for transfers between devices: 21 us -> 0 us
  starting transfers between devices: 7 us -> 0 us
  other arithmetic: 5.86 us -> 0 us
  matrix products: 3.06 us -> 0 us
  local copies, waits for them, and re-layouts: 5.75 us -> 6.82 us
    pallas_call x1, Pallas kernels: 54.2 us -> 77.4 us  [whole_step(): pl.pallas_call(project_kernel, out_shape=(jax.ShapeDtypeStruct((group, he...]
    all_to_all x2 -> x0, waiting for transfers between devices: 21 us -> none  [the longest x1 15 us: body(): lax.all_to_all(partial, ('blk', 'rep'), split_axis=0, concat_axis=0, tile...]
    all_to_all x2 -> x0, starting transfers between devices: 7 us -> none  [the longest x1 3.54 us: body(): lax.all_to_all(partial, ('blk', 'rep'), split_axis=0, concat_axis=0, tile...]
    dot_general x3 -> x0, matrix products: 3.06 us -> none  [the longest x1 1.03 us: body(): jnp.einsum('kaqht,tkd->kaqhd', weights.astype(jnp.bfloat16), values, pref...]
    reduce_sum x5 -> x0, other arithmetic: 2.93 us -> none  [the longest x1 1.04 us: body(): total = jnp.sum(weights, axis=-1)]
    unnamed x11 -> x8, local copies, waits for them, and re-layouts: 2.56 us -> 4.54 us
  transfers between devices with their start and end apart: 2 -> 0, of which waited for: 2 -> 0; matrix products, arithmetic and copies ran while one was open for 7% -> 0% of each run, Pallas kernels for 0% -> 0%
where the time goes in v3:
time: 85.1 us; the launch traced here: 84.9 us
  Pallas kernels  77.4 us (91%)
  local copies, waits for them, and re-layouts  6.82 us (8%)
    pallas_call x1, Pallas kernels, whole_step(): pl.pallas_call(project_kernel, out_shape=(jax.ShapeDtypeStruct((group, he...  77.4 us
    unnamed x8, local copies, waits for them, and re-layouts  4.54 us

profile of v3, /device:TPU:0, one launch (start us, length us, event | category | flops | bytes accessed | tf_op | source)
XLA Modules:
  0.0 84.9 jit_solution(14097302816665986404)
XLA Ops:
  0.6 0.7 copy.17
  1.3 0.7 copy.14.owner_ref
  2.1 0.8 copy.13.merge_ref
  2.8 0.9 %reshape.26 = bf16[2,4,4,8,128]{4,3,2,1,0:T(8,128)(2,1)S(1)} reshape(bf16[1,8,4,1024]{3,2,1,0:T(4,128)(2,1)} %param.16) | data formatting | bytes 131072 | tf_op jit(solution)/shard_map/reshape | solution.py:648
  3.7 0.0 copy-start
  3.7 0.0 copy-start.1
  3.7 2.0 %copy.20 = bf16[128,8,4,256]{3,1,0,2:T(8,128)(2,1)S(1)} copy(bf16[128,8,4,256]{3,2,1,0:T(4,128)(2,1)} %param.15) | data formatting | bytes 4194304 | tf_op args[6]
  5.7 0.1 copy-done
  5.9 0.0 copy-done.1
  5.9 77.4 %shard_map.104 = (bf16[128,128]{1,0:T(8,128)(2,1)S(1)}, bf16[4,48,1024]{2,1,0:T(8,128)(2,1)S(1)}) custom-call(bf16[192,5120]{1,0:T(8,128)(2,1)S(1)} %copy-done, bf16[1280,2048]{1,0:T(8,128)(2,1)} %weight_ref.1, bf16[2048,2048]{1,0:T(8,128)(2,1)} %kv_ref.1, f32[1,1024]{1,0:T(1,128)S(1)} %bitcast.21, bf16[2,128,128]{2,1,0:T(8,128)(2,1)S(1)} %bitcast.20, ...), custom_call_target="tpu_custom_call" | custom-call | flops 10468982784 | bytes 15597568 | tf_op jit(solution)/shard_map/pallas_call | solution.py:584
  83.3 0.6 copy.21
  83.9 0.9 %copy.16 = bf16[24,8,4,256]{3,2,1,0:T(4,128)(2,1)} copy(bf16[24,8,4,256]{3,1,2,0:T(8,128)(2,1)S(1)} %bitcast.19) | data formatting | bytes 786432
  (2 shorter events, 0.0 us)
Async XLA Ops:
  3.7 2.2 %copy-start = (bf16[192,5120]{1,0:T(8,128)(2,1)S(1)}, bf16[192,5120]{1,0:T(8,128)(2,1)}, u32[]{:S(2)}) copy-start(bf16[192,5120]{1,0:T(8,128)(2,1)} %rows_ref.1) | copy-start | bytes 5898244
  3.7 2.2 %copy-start.1 = (s32[4,32]{1,0:T(4,128)S(1)}, s32[4,32]{1,0:T(4,128)}, u32[]{:S(2)}) copy-start(s32[4,32]{1,0:T(4,128)} %retrieved_ref.1) | copy-start | bytes 1540

commit v4 on v3

--- a/solution.py
+++ b/solution.py
@@ -27,7 +27,7 @@
 
 
 TILE = 512
-ORDER = (0, 2, 3, 1)
+ORDER = (0, 3, 2, 1)
 VMEM_BYTES = 48 * 1024 * 1024
 
 
@@ -150,14 +150,9 @@
         started.append(copy)
         return copy
 
-    asking = [
-        begin(
-            remote(queries_ref, asked.at[k], query_send.at[k], query_recv.at[k], to_blk(k))
-        )
-        for k in (1, 2, 3)
-    ]
-    over_blk = {}
-    for k in ORDER[1:]:
+    over_blk, asking, ask_again = {}, {}, {}
+
+    def send_features(k):
         over_blk[k] = begin(
             remote(
                 rows_ref.at[own_rows, feature_columns(k)],
@@ -168,6 +163,30 @@
             )
         )
 
+    def send_queries():
+        for k in (1, 2, 3):
+            asking[k] = begin(
+                remote(
+                    queries_ref.at[rep],
+                    asked.at[k, rep],
+                    query_send.at[0, k],
+                    query_recv.at[0, k],
+                    to_blk(k),
+                )
+            )
+
+    def pass_queries():
+        for k in (1, 2, 3):
+            asking[k].wait_recv()
+            piece = asked.at[k, rep]
+            ask_again[k] = begin(
+                remote(piece, piece, query_send.at[1, k], query_recv.at[1, k], to_rep)
+            )
+
+    send_features(ORDER[1])
+    send_features(ORDER[2])
+    send_features(ORDER[3])
+
     over_head, over_rep, last_rep = {}, {}, {}
 
     def pass_quarter(k):
@@ -200,6 +219,7 @@
             ).astype(jnp.bfloat16)
 
         if k == 0:
+            send_queries()
             load_kv.wait()
 
         @pl.loop(0, cols // TILE)
@@ -246,16 +266,22 @@
         own_sums[k] = (
             half_sums[k, :, own_cols].astype(jnp.float32) + got_head[k].astype(jnp.float32)
         ).astype(jnp.bfloat16)
-        if k != 0:
-            by_blk[k] = begin(
-                remote(
-                    own_sums.at[k],
-                    got_blk.at[k],
-                    sum_send.at[2, k],
-                    sum_recv.at[2, k],
-                    to_blk(k),
-                )
-            )
+        if k == 0:
+            return
+        if k == 2:
+            by_blk[3].wait_recv()
+            own_sums[2] = (
+                own_sums[2].astype(jnp.float32) + got_blk[3].astype(jnp.float32)
+            ).astype(jnp.bfloat16)
+        by_blk[k] = begin(
+            remote(
+                own_sums.at[k],
+                got_blk.at[k],
+                sum_send.at[2, k],
+                sum_recv.at[2, k],
+                to_blk(2 if k == 2 else 1),
+            )
+        )
 
     heads = stored.shape[0]
     stored_rows = stored.shape[1]
@@ -437,11 +463,12 @@
     pass_second(second)
     select = prepare()
     asked[0] = queries_ref[...]
-    for copy in asking:
+    send_head(first)
+    pass_queries()
+    pass_quarter(third)
+    load_stored.wait()
+    for copy in ask_again.values():
         copy.wait_recv()
-    load_stored.wait()
-    send_head(first)
-    pass_quarter(third)
     attend_stored()
     send_stored()
     have_rows(second)
@@ -466,7 +493,7 @@
     send_blk(fourth)
 
     total = own_sums[0].astype(floats) + bias_ref[...]
-    for k in ORDER[1:]:
+    for k in (2, 1):
         by_blk[k].wait_recv()
         total = total + got_blk[k].astype(floats)
     new_rows[0] = total.astype(jnp.bfloat16)
@@ -478,6 +505,19 @@
         .astype(jnp.bfloat16)
         .reshape(units.shape)
     )
+    relayout = []
+    for k in ORDER[1:]:
+        relayout.append(
+            begin(
+                remote(
+                    units.at[partner(block, k)],
+                    got_units.at[k],
+                    end_send.at[2, k],
+                    end_recv.at[2, k],
+                    to_blk(k),
+                )
+            )
+        )
     share.wait_recv()
     attend_new()
     ended = []
@@ -503,19 +543,6 @@
                         to_blk(k),
                     )
                 ),
-            )
-        )
-    relayout = []
-    for k in ORDER[1:]:
-        relayout.append(
-            begin(
-                remote(
-                    units.at[partner(block, k)],
-                    got_units.at[k],
-                    end_send.at[2, k],
-                    end_recv.at[2, k],
-                    to_blk(k),
-                )
             )
         )
     memory_ref[block] = units[block]
@@ -580,7 +607,7 @@
         ((4, 8, head_size), wide),
         ((4, 8, head_size), wide),
     ]
-    semaphores = [(4,), (4, 4), (4, 4), (3, 4), (3, 4), (4,), (4,), (4,), (4,), (3, 4), (3, 4)]
+    semaphores = [(4,), (4, 4), (4, 4), (3, 4), (3, 4), (2, 4), (2, 4), (4,), (4,), (3, 4), (3, 4)]
     return pl.pallas_call(
         project_kernel,
         out_shape=(

time: 85.1 us -> 80 us (0.940)
  Pallas kernels: 77.4 us -> 72.3 us
    pallas_call x1, Pallas kernels: 77.4 us -> 72.3 us  [whole_step(): pl.pallas_call(project_kernel, out_shape=(jax.ShapeDtypeStruct((group, he...]
where the time goes in v4:
time: 80 us; the launch traced here: 79.8 us
  Pallas kernels  72.3 us (90%)
  local copies, waits for them, and re-layouts  6.82 us (9%)
    pallas_call x1, Pallas kernels, whole_step(): pl.pallas_call(project_kernel, out_shape=(jax.ShapeDtypeStruct((group, he...  72.3 us
    unnamed x8, local copies, waits for them, and re-layouts  4.54 us

profile of v4, /device:TPU:0, one launch (start us, length us, event | category | flops | bytes accessed | tf_op | source)
XLA Modules:
  0.0 79.8 jit_solution(17797546279034301621)
XLA Ops:
  0.6 0.7 copy.17
  1.3 0.7 copy.14.owner_ref
  2.1 0.8 copy.13.merge_ref
  2.8 0.9 %reshape.26 = bf16[2,4,4,8,128]{4,3,2,1,0:T(8,128)(2,1)S(1)} reshape(bf16[1,8,4,1024]{3,2,1,0:T(4,128)(2,1)} %param.16) | data formatting | bytes 131072 | tf_op jit(solution)/shard_map/reshape | solution.py:675
  3.7 0.0 copy-start
  3.7 0.0 copy-start.1
  3.7 2.0 %copy.20 = bf16[128,8,4,256]{3,1,0,2:T(8,128)(2,1)S(1)} copy(bf16[128,8,4,256]{3,2,1,0:T(4,128)(2,1)} %param.15) | data formatting | bytes 4194304 | tf_op args[6]
  5.7 0.1 copy-done
  5.9 0.0 copy-done.1
  5.9 72.3 %shard_map.104 = (bf16[128,128]{1,0:T(8,128)(2,1)S(1)}, bf16[4,48,1024]{2,1,0:T(8,128)(2,1)S(1)}) custom-call(bf16[192,5120]{1,0:T(8,128)(2,1)S(1)} %copy-done, bf16[1280,2048]{1,0:T(8,128)(2,1)} %weight_ref.1, bf16[2048,2048]{1,0:T(8,128)(2,1)} %kv_ref.1, f32[1,1024]{1,0:T(1,128)S(1)} %bitcast.21, bf16[2,128,128]{2,1,0:T(8,128)(2,1)S(1)} %bitcast.20, ...), custom_call_target="tpu_custom_call" | custom-call | flops 10468982784 | bytes 15597568 | tf_op jit(solution)/shard_map/pallas_call | solution.py:611
  78.2 0.6 copy.21
  78.8 0.9 %copy.16 = bf16[24,8,4,256]{3,2,1,0:T(4,128)(2,1)} copy(bf16[24,8,4,256]{3,1,2,0:T(8,128)(2,1)S(1)} %bitcast.19) | data formatting | bytes 786432
  (2 shorter events, 0.0 us)
Async XLA Ops:
  3.7 2.2 %copy-start = (bf16[192,5120]{1,0:T(8,128)(2,1)S(1)}, bf16[192,5120]{1,0:T(8,128)(2,1)}, u32[]{:S(2)}) copy-start(bf16[192,5120]{1,0:T(8,128)(2,1)} %rows_ref.1) | copy-start | bytes 5898244
  3.7 2.2 %copy-start.1 = (s32[4,32]{1,0:T(4,128)S(1)}, s32[4,32]{1,0:T(4,128)}, u32[]{:S(2)}) copy-start(s32[4,32]{1,0:T(4,128)} %retrieved_ref.1) | copy-start | bytes 1540

commit v5 on v4

--- a/solution.py
+++ b/solution.py
@@ -348,11 +348,11 @@
         new_mask[0, 0:4, 0:half] = listed(base + unit_row.astype(jnp.int32))
         return select
 
-    def attend_stored():
+    def attend_stored(start_head, stop_head):
         ids = place * (stored_rows // UNIT_TOK) + iota((1, stored_rows), 1) // UNIT_TOK
         mask = row_mask(listed(ids), 2 * ask_rows) > 0.0
 
-        @pl.loop(0, heads)
+        @pl.loop(start_head, stop_head)
         def _(h):
             at = pl.ds(pl.multiple_of(h * ask_rows, ask_rows), ask_rows)
             query = jnp.concatenate(
@@ -381,13 +381,12 @@
                     old_out[r, k, at, :] = output[start : start + ask_rows]
                     old_log[r, k, at, :] = logs[start : start + ask_rows]
 
+    old_parts = []
+
+    def send_stored():
         old_out_send[...] = old_out[1 - rep].astype(jnp.bfloat16)
         for k in range(4):
             old_log_send[k] = flat_log(old_log[1 - rep, k])
-
-    old_parts = []
-
-    def send_stored():
         for i, (src, dst) in enumerate(
             (
                 (old_out_send, old_out_got),
@@ -466,11 +465,6 @@
     send_head(first)
     pass_queries()
     pass_quarter(third)
-    load_stored.wait()
-    for copy in ask_again.values():
-        copy.wait_recv()
-    attend_stored()
-    send_stored()
     have_rows(second)
     multiply(second)
     send_rep(second)
@@ -489,8 +483,13 @@
     send_rep(fourth)
     send_blk(third)
     send_head(fourth)
-    merge_stored()
+    load_stored.wait()
+    for copy in ask_again.values():
+        copy.wait_recv()
+    attend_stored(0, heads // 2)
     send_blk(fourth)
+    attend_stored(heads // 2, heads)
+    send_stored()
 
     total = own_sums[0].astype(floats) + bias_ref[...]
     for k in (2, 1):
@@ -518,6 +517,7 @@
                 )
             )
         )
+    merge_stored()
     share.wait_recv()
     attend_new()
     ended = []

time: 80 us -> 76.5 us (0.956)
  Pallas kernels: 72.3 us -> 68.7 us
    pallas_call x1, Pallas kernels: 72.3 us -> 68.7 us  [whole_step(): pl.pallas_call(project_kernel, out_shape=(jax.ShapeDtypeStruct((group, he...]
where the time goes in v5:
time: 76.5 us; the launch traced here: 76.2 us
  Pallas kernels  68.7 us (90%)
  local copies, waits for them, and re-layouts  6.82 us (9%)
    pallas_call x1, Pallas kernels, whole_step(): pl.pallas_call(project_kernel, out_shape=(jax.ShapeDtypeStruct((group, he...  68.7 us
    unnamed x8, local copies, waits for them, and re-layouts  4.54 us

profile of v5, /device:TPU:0, one launch (start us, length us, event | category | flops | bytes accessed | tf_op | source)
XLA Modules:
  0.0 76.2 jit_solution(3863164811027423334)
XLA Ops:
  0.6 0.7 copy.17
  1.3 0.7 copy.14.owner_ref
  2.1 0.8 copy.13.merge_ref
  2.8 0.9 %reshape.26 = bf16[2,4,4,8,128]{4,3,2,1,0:T(8,128)(2,1)S(1)} reshape(bf16[1,8,4,1024]{3,2,1,0:T(4,128)(2,1)} %param.16) | data formatting | bytes 131072 | tf_op jit(solution)/shard_map/reshape | solution.py:675
  3.7 0.0 copy-start
  3.7 0.0 copy-start.1
  3.7 2.0 %copy.20 = bf16[128,8,4,256]{3,1,0,2:T(8,128)(2,1)S(1)} copy(bf16[128,8,4,256]{3,2,1,0:T(4,128)(2,1)} %param.15) | data formatting | bytes 4194304 | tf_op args[6]
  5.7 0.1 copy-done
  5.9 0.0 copy-done.1
  5.9 68.7 %shard_map.104 = (bf16[128,128]{1,0:T(8,128)(2,1)S(1)}, bf16[4,48,1024]{2,1,0:T(8,128)(2,1)S(1)}) custom-call(bf16[192,5120]{1,0:T(8,128)(2,1)S(1)} %copy-done, bf16[1280,2048]{1,0:T(8,128)(2,1)} %weight_ref.1, bf16[2048,2048]{1,0:T(8,128)(2,1)} %kv_ref.1, f32[1,1024]{1,0:T(1,128)S(1)} %bitcast.21, bf16[2,128,128]{2,1,0:T(8,128)(2,1)S(1)} %bitcast.20, ...), custom_call_target="tpu_custom_call" | custom-call | flops 10468982784 | bytes 15597568 | tf_op jit(solution)/shard_map/pallas_call | solution.py:611
  74.7 0.6 copy.21
  75.3 0.9 %copy.16 = bf16[24,8,4,256]{3,2,1,0:T(4,128)(2,1)} copy(bf16[24,8,4,256]{3,1,2,0:T(8,128)(2,1)S(1)} %bitcast.19) | data formatting | bytes 786432
  (2 shorter events, 0.0 us)
Async XLA Ops:
  3.7 2.2 %copy-start = (bf16[192,5120]{1,0:T(8,128)(2,1)S(1)}, bf16[192,5120]{1,0:T(8,128)(2,1)}, u32[]{:S(2)}) copy-start(bf16[192,5120]{1,0:T(8,128)(2,1)} %rows_ref.1) | copy-start | bytes 5898244
  3.7 2.2 %copy-start.1 = (s32[4,32]{1,0:T(4,128)S(1)}, s32[4,32]{1,0:T(4,128)}, u32[]{:S(2)}) copy-start(s32[4,32]{1,0:T(4,128)} %retrieved_ref.1) | copy-start | bytes 1540
